TPU v7x, 512 devices: a whole 4x8x8 slice. The times are simulated.
512 devices in a mesh: group: 32 (over z, y_hi), blk: 16 (over y_lo, x, core).
Axes of the slice: x: 4, y: 8 (y_hi: 4, y_lo: 2; y = y_hi * 2 + y_lo), z: 8, core: 2. Of those that a mesh axis runs over, the one named last changes fastest.
Arguments:
- right_side: float32 [96, 32768], P(None, ('group', 'blk')), may hold values from -6 to 6
- positions: float32 [3, 32768], P(None, ('group', 'blk')), may hold values from -0.5 to 0.5
- wavenumber: float32 [1], replicated, may hold values from 12 to 24
Outputs:
- solution_field: float32 [96, 32768], P(None, ('group', 'blk'))
- residual: float32 [96, 32768], P(None, ('group', 'blk'))
All inputs are finite; a program needn't handle non-finite values.
Results may differ from a plain program's by a relative error of at most 0.0003.
Values sent between devices are 32-bit elements; how exact they have to be, the bound alone decides.
No kernel may reach another device: no remote copies, remote signals or barrier semaphores. Data moves between devices by JAX's collectives and lax.ppermute only.
A program may use at most 64 MiB of HBM per device.

v0:
```python
import jax
import jax.numpy as jnp
from jax import lax
from jax.sharding import PartitionSpec as P

ITERS = 2


def kernel_block(cols, rows, kappa):
    delta_x = cols[0][:, None] - rows[0][None, :]
    delta_y = cols[1][:, None] - rows[1][None, :]
    delta_z = cols[2][:, None] - rows[2][None, :]
    dist = jnp.sqrt(delta_x * delta_x + delta_y * delta_y + delta_z * delta_z)
    return jnp.sinc(kappa * dist / jnp.pi)


def block_width(width):
    for cand in (512, 256, 128):
        return cand
    return width


def add_columns(total, rows, cols, dirs, kappa):
    width = cols.shape[1]
    step = block_width(width)
    count = width // step

    def one_block(index, acc):
        start = (index * step).astype(jnp.int32)
        col_part = lax.dynamic_slice_in_dim(cols, start, step, 1)
        dir_part = lax.dynamic_slice_in_dim(dirs, start, step, 1)
        return acc + jnp.dot(
            dir_part,
            kernel_block(col_part, rows, kappa),
            preferred_element_type=jnp.float32,
            precision=lax.Precision.HIGHEST,
        )

    return lax.fori_loop(0, count, one_block, total)


def squares(vector):
    return lax.psum(jnp.sum(vector * vector, axis=1), ("group", "blk"))


def local(right_side, positions, wavenumber):
    kappa = wavenumber[0]
    row_points = lax.all_gather(positions, "blk", axis=1, tiled=True)
    col_points = lax.all_gather(positions, "group", axis=1, tiled=True)
    solution_field = jnp.zeros_like(right_side)
    residual = right_side
    direction = right_side
    norm_now = squares(residual)
    for step in range(ITERS):
        empty = jnp.zeros((direction.shape[0], row_points.shape[1]), jnp.float32)
        partial_sum = add_columns(
            empty,
            row_points,
            col_points,
            lax.all_gather(direction, "group", axis=1, tiled=True),
            kappa,
        )
        image = (
            lax.psum_scatter(partial_sum, "blk", scatter_dimension=1, tiled=True) + 0.01 * direction
        )
        alpha = norm_now / lax.psum(jnp.sum(direction * image, axis=1), ("group", "blk"))
        solution_field = solution_field + alpha[:, None] * direction
        residual = residual - alpha[:, None] * image
        if step + 1 < ITERS:
            norm_next = squares(residual)
            direction = residual + (norm_next / norm_now)[:, None] * direction
            norm_now = norm_next
    return (solution_field, residual)


def solution(mesh):
    return jax.shard_map(
        local,
        mesh=mesh,
        in_specs=(P(None, ("group", "blk")), P(None, ("group", "blk")), P()),
        out_specs=(P(None, ("group", "blk")), P(None, ("group", "blk"))),
        check_vma=False,
    )
```

profile of v0, /device:TPU:1, one launch (start us, length us, event | category | flops | bytes accessed | tf_op | source)
XLA Modules:
  0.0 751.3 jit_solution(4734433570469555179)
XLA Ops:
  7.2 0.0 reduce-scatter.3.cloned.1.call-start
  7.2 75.2 %all-gather = f32[32,64,3]{1,2,0:T(4,128)S(1)} all-gather(f32[1,64,3]{1,2,0:T(4,128)} %bitcast.60), channel_id=1, replica_groups=mesh['group'=32,'blk'=16] {'group'}, dimensions={0}, use_global_device_ids=true | all-gather | bytes 25344 | tf_op jit(solution)/shard_map/all_gather | solution.py:49
  82.5 33.7 %all-gather.1 = f32[16,64,3]{1,2,0:T(4,128)S(1)} all-gather(f32[1,64,3]{1,2,0:T(4,128)} %bitcast.61), channel_id=1, replica_groups=mesh['group'=32,'blk'=16] {'blk'}, dimensions={0}, use_global_device_ids=true | all-gather | bytes 13056 | tf_op jit(solution)/shard_map/all_gather | solution.py:48
  116.2 0.1 reshape.14
  116.3 0.1 reshape.16
  116.4 69.8 %all_gather.12 = f32[96,2048]{0,1:T(8,128)S(1)} all-gather(f32[96,64]{0,1:T(8,128)} %param.8), channel_id=1, replica_groups=mesh['group'=32,'blk'=16] {'group'}, dimensions={1}, use_global_device_ids=true | all-gather | bytes 811008 | tf_op jit(solution)/shard_map/all_gather | solution.py:60
  186.1 0.3 copy.17
  186.4 22.9 %while.28 = (s32[]{:T(128)}, f32[96,1024]{1,0:T(8,128)S(1)}, f32[96,2048]{1,0:T(8,128)S(1)}, f32[]{:T(128)}, f32[3,2048]{1,0:T(4,128)S(1)}, /*index=5*/f32[3,102...) while((s32[]{:T(128)}, f32[96,1024]{1,0:T(8,128)S(1)}, ...), condition=%wide.region_3.5_spmd.clone, body=%wide.region_2.4_spmd.clone.sunk | while | flops 626720768 | bytes 1038553 | solution.py:39
  186.5 0.1 constant_dynamic-slice_fusion.4
  186.6 5.6 fusion.113
  192.2 0.1 constant_dynamic-slice_fusion.4
  192.3 5.6 fusion.113
  197.9 0.1 constant_dynamic-slice_fusion.4
  198.0 5.6 fusion.113
  203.7 0.1 constant_dynamic-slice_fusion.4
  203.8 5.6 fusion.113
  209.4 0.0 copy-start
  209.4 1.0 copy.18
  210.4 0.0 reduce-scatter.3.cloned.1.call-update
  210.4 0.0 reduce-scatter.5.cloned.1.call-start
  210.5 68.4 %reduce-scatter.3.cloned.1.call-done = f32[96,64]{0,1:T(8,128)} async-done(((f32[96,1024]{0,1:T(8,128)}), f32[96,64]{0,1:T(8,128)}) %reduce-scatter.3.cloned.1.call-update) | async-done | bytes 24592 | tf_op jit(solution)/shard_map/reduce_scatter | solution.py:64
  278.8 0.0 copy-done
  278.9 0.8 multiply_reduce_fusion.2
  279.6 100.2 %all-reduce = (f32[96]{0:T(128)S(1)}, f32[96]{0:T(128)S(1)}) all-reduce(f32[96]{0:T(128)S(1)} %get-tuple-element.296, f32[96]{0:T(128)S(1)} %get-tuple-element.295), channel_id=1, replica_groups=mesh['group'=32,'blk'=16] {'group','blk'}, use_global_device_ids=true, to_apply=%region_1.0 | all-reduce | flops 192 | bytes 1536 | tf_op jit(solution)/shard_map/psum | solution.py:43
  379.9 0.8 multiply_reduce_fusion.1
  380.7 94.1 %psum.30 = f32[96]{0:T(128)S(1)} all-reduce(f32[96]{0:T(128)S(1)} %multiply_reduce_fusion.1), channel_id=1, replica_groups=mesh['group'=32,'blk'=16] {'group','blk'}, use_global_device_ids=true, to_apply=%region_8.10 | all-reduce | flops 96 | bytes 768 | tf_op jit(solution)/shard_map/psum | solution.py:43
  474.8 0.8 multiply_add_fusion.4
  475.5 71.4 %all_gather.15 = f32[96,2048]{0,1:T(8,128)S(1)} all-gather(f32[96,64]{0,1:T(8,128)S(1)} %multiply_add_fusion.4), channel_id=1, replica_groups=mesh['group'=32,'blk'=16] {'group'}, dimensions={1}, use_global_device_ids=true | all-gather | bytes 811008 | tf_op jit(solution)/shard_map/all_gather | solution.py:60
  547.0 0.3 copy.19
  547.3 22.9 %while.29 = (s32[]{:T(128)}, f32[96,1024]{1,0:T(8,128)S(1)}, f32[96,2048]{1,0:T(8,128)S(1)}, f32[]{:T(128)}, f32[3,2048]{1,0:T(4,128)S(1)}, /*index=5*/f32[3,102...) while((s32[]{:T(128)}, f32[96,1024]{1,0:T(8,128)S(1)}, ...), condition=%wide.region_10.12_spmd.clone, body=%wide.region_9.11_spmd.clone.sunk | while | flops 626720768 | bytes 1038553 | solution.py:39
  547.3 0.1 constant_dynamic-slice_fusion.5
  547.4 5.6 fusion.117
  553.0 0.1 constant_dynamic-slice_fusion.5
  553.1 5.6 fusion.117
  558.8 0.1 constant_dynamic-slice_fusion.5
  558.9 5.6 fusion.117
  564.5 0.1 constant_dynamic-slice_fusion.5
  564.6 5.6 fusion.117
  570.2 0.0 copy-start.1
  570.2 1.0 copy.20
  571.2 0.0 reduce-scatter.5.cloned.1.call-update
  571.2 70.8 %reduce-scatter.5.cloned.1.call-done = f32[96,64]{0,1:T(8,128)} async-done(((f32[96,1024]{0,1:T(8,128)}), f32[96,64]{0,1:T(8,128)}) %reduce-scatter.5.cloned.1.call-update) | async-done | bytes 24592 | tf_op jit(solution)/shard_map/reduce_scatter | solution.py:64
  642.0 0.8 multiply_reduce_fusion
  642.8 100.3 %psum.31 = f32[96]{0:T(128)S(1)} all-reduce(f32[96]{0:T(128)S(1)} %multiply_reduce_fusion), channel_id=1, replica_groups=mesh['group'=32,'blk'=16] {'group','blk'}, use_global_device_ids=true, to_apply=%region_13.15 | all-reduce | flops 96 | bytes 768 | tf_op jit(solution)/shard_map/psum | solution.py:66
  743.1 0.0 copy-done.1
  743.1 1.4 multiply_subtract_fusion
  (15 shorter events, 0.1 us)
Async XLA Ops:
  7.2 271.7 %reduce-scatter.3.cloned.1.call-start = ((), (), s32[]{:S(2)}) async-start(), calls=%async_computation.2 | async-start | bytes 557056 | tf_op jit(solution)/shard_map/reduce_scatter | solution.py:64
  209.4 69.5 %copy-start = (f32[96,64]{0,1:T(8,128)S(1)}, f32[96,64]{0,1:T(8,128)}, u32[]{:S(2)}) copy-start(f32[96,64]{0,1:T(8,128)} %param.8) | copy-start | bytes 73732
  210.4 431.6 %reduce-scatter.5.cloned.1.call-start = ((), (), s32[]{:S(2)}) async-start(), calls=%async_computation.3 | async-start | bytes 557056 | tf_op jit(solution)/shard_map/reduce_scatter | solution.py:64
  570.2 172.9 %copy-start.1 = (f32[96,64]{0,1:T(8,128)S(1)}, f32[96,64]{0,1:T(8,128)}, u32[]{:S(2)}) copy-start(f32[96,64]{0,1:T(8,128)} %reduce-scatter.3.cloned.1.call-done) | copy-start | bytes 73732
Sparse Core Ops, SparseCore 0:
  210.5 68.2 reduce-scatter.2
  571.3 70.6 reduce-scatter.4
where the time goes:
time: 752 us; the launch traced here: 751 us
  blocking collectives  545 us (72%)
  waiting for transfers between devices  139 us (18%)
  matrix products  44.7 us (6%)
  between operations  14.1 us (2%)
    psum x2, blocking collectives, squares(): return lax.psum(jnp.sum(vector * vector, axis=1), ('group', 'blk'))  194 us
    all_gather x2, blocking collectives, local(): lax.all_gather(direction, 'group', axis=1, tiled=True)  141 us
    reduce_scatter x2, waiting for transfers between devices, local(): lax.psum_scatter(partial_sum, 'blk', scatter_dimension=1, tiled=True)  139 us
    psum x1, blocking collectives, local(): lax.psum(jnp.sum(direction * image, axis=1), ('group', 'blk'))  100 us
    all_gather x1, blocking collectives, local(): col_points = lax.all_gather(positions, 'group', axis=1, tiled=True)  75.2 us
    dot_general x8, matrix products, one_block(): jnp.dot(dir_part, kernel_block(col_part, rows, kappa), preferred_element_...  44.7 us
    all_gather x1, blocking collectives, local(): row_points = lax.all_gather(positions, 'blk', axis=1, tiled=True)  33.7 us
  transfers between devices with their start and end apart: 2, of which 2 were waited for; matrix products, arithmetic and copies ran while one was open for 0% of the time, Pallas kernels for 0%

commit v1 on v0

v1 whole, which is shorter than its diff:
```python
import math

import jax
import jax.numpy as jnp
from jax import lax
from jax.experimental import pallas as pl
from jax.experimental.pallas import tpu as pltpu
from jax.sharding import PartitionSpec as P

LANES = 128
MICS = 64
EXTRA = 8
STEP = 256
CHUNK = 128
SHIFT = 0.01
BF16 = jnp.bfloat16
F32 = jnp.float32
SINC = (
    0.9999999403953552,
    -6.579718112945557,
    12.987034797668457,
    -12.193572998046875,
    6.579925060272217,
    -1.9848603010177612,
)
PARAMS = pltpu.CompilerParams(vmem_limit_bytes=48 * 1024 * 1024)


def dot(left, right):
    return lax.dot_general(left, right, (((1,), (0,)), ((), ())), preferred_element_type=F32)


def rounded(value):
    return value.astype(BF16).astype(F32)


def lane_of(shape):
    return lax.broadcasted_iota(jnp.int32, shape, len(shape) - 1)


def frames_only(value, frames):
    return jnp.where(lane_of(value.shape) < frames, value, 0.0)


def wide(value):
    return jnp.concatenate(
        [value, jnp.zeros((value.shape[0], LANES - value.shape[1]), F32)], axis=1
    )


def halves(value):
    high = value.astype(BF16)
    return high, (value - high.astype(F32)).astype(BF16)


def start_kernel(field_ref, points_ref, wave_ref, col_ref, row_ref):
    frames = field_ref.shape[1]
    scaled = points_ref[...] * (wave_ref[0] * (0.5 / math.pi))
    squares = jnp.sum(scaled * scaled, axis=1, keepdims=True)

    def thirds(value):
        one = rounded(value)
        two = rounded(value - one)
        return one, two, rounded(value - one - two)

    rows, cols = [], []
    for axis in range(3):
        one, two, three = thirds(scaled[:, axis : axis + 1])
        rows += [one, one, two, two, one, three]
        cols += [-2.0 * v for v in (one, two, one, two, three, one)]
    rows += list(thirds(squares)) + [1.0, 1.0, 1.0]
    cols += [1.0, 1.0, 1.0] + list(thirds(squares))

    field = wide(field_ref[...])
    lane = lane_of(field.shape)
    row_block = col_block = field
    for place, (row, col) in enumerate(zip(rows, cols)):
        row_block = jnp.where(lane == frames + place, row, row_block)
        col_block = jnp.where(lane == frames + place, col, col_block)
    col_ref[...] = jnp.broadcast_to(col_block[None], col_ref.shape)
    row_ref[...] = jnp.broadcast_to(row_block[None], row_ref.shape)


def spread(out_ref, value, sums):
    out_ref[:, :MICS, :] = value.reshape(out_ref.shape[0], MICS, LANES)
    out_ref[:, MICS:, :] = jnp.broadcast_to(sums[None], (out_ref.shape[0], EXTRA, LANES))


def stacked(*rows):
    return jnp.concatenate(
        list(rows) + [jnp.zeros((EXTRA - len(rows), LANES), F32)], axis=0
    )


def product(high_ref, low_ref, weights_ref):
    both = dot(high_ref[...], weights_ref[...])
    rest = dot(low_ref[...], weights_ref[:, :LANES])
    return both[:, :LANES] + both[:, LANES:] + rest


def first_kernel(
    frames, col_ref, row_ref, field_ref, out_ref, high_ref, low_ref, weights_ref, col_f, row_f
):
    cols, rows = col_f.shape[0], row_f.shape[0]

    def factors(value):
        return jnp.where(lane_of(value.shape) < frames, 0.0, value).astype(BF16)

    def place_col(index, carry):
        at = pl.ds(pl.multiple_of(index * MICS, MICS), MICS)
        block = col_ref[index]
        col_f[at, :] = factors(block)
        high, low = halves(frames_only(block, frames))
        weights_ref[at, :LANES] = high
        weights_ref[at, LANES:] = low
        return carry

    lax.fori_loop(0, cols // MICS, place_col, 0)
    row_f[...] = factors(row_ref[...].reshape(rows, LANES))

    def columns(index, carry):
        at = pl.ds(pl.multiple_of(index * STEP, STEP), STEP)
        right = col_f[at, :]
        for first in range(0, rows, CHUNK):
            turns2 = lax.dot_general(
                row_f[first : first + CHUNK, :],
                right,
                (((1,), (1,)), ((), ())),
                preferred_element_type=F32,
            )
            turns2 = jnp.maximum(turns2, 1e-12)
            inverse = lax.rsqrt(turns2)
            turns = turns2 * inverse
            part = turns - lax.round(turns, lax.RoundingMethod.TO_NEAREST_EVEN)
            square = part * part
            value = jnp.full_like(square, SINC[-1])
            for factor in SINC[-2::-1]:
                value = value * square + factor
            high, low = halves(value * (part * inverse))
            high_ref[first : first + CHUNK, at] = high
            low_ref[first : first + CHUNK, at] = low
        return carry

    lax.fori_loop(0, cols // STEP, columns, 0)
    result = product(high_ref, low_ref, weights_ref)
    field_rows = frames_only(row_ref[...].reshape(rows, LANES), frames)
    own = field_ref[...]
    spread(
        out_ref,
        result,
        stacked(
            jnp.sum(field_rows * result, axis=0, keepdims=True),
            wide(jnp.sum(own * own, axis=0, keepdims=True)),
        ),
    )


def image_kernel(got_ref, field_ref, image_ref, send_ref):
    total = jnp.sum(got_ref[...], axis=0)
    image = total[:MICS] + SHIFT * wide(field_ref[...])
    image_ref[...] = image
    send_ref[:, :MICS, :] = jnp.broadcast_to(image[None], (send_ref.shape[0], MICS, LANES))
    send_ref[:, MICS:, :] = jnp.broadcast_to(
        total[MICS:][None], (send_ref.shape[0], EXTRA, LANES)
    )


def second_kernel(frames, got_ref, col_ref, high_ref, low_ref, out_ref, sums_ref, weights_ref):
    sums = jnp.sum(got_ref[:, MICS:, :], axis=0)
    norm = sums[1:2]
    alpha = norm / (sums[0:1] + SHIFT * norm)

    def place(index, total):
        at = pl.ds(pl.multiple_of(index * MICS, MICS), MICS)
        residual = frames_only(col_ref[index] - alpha * got_ref[index, :MICS, :], frames)
        high, low = halves(residual)
        weights_ref[at, :LANES] = high
        weights_ref[at, LANES:] = low
        return total + jnp.sum((residual * residual).reshape(-1, 8, LANES), axis=0)

    squares = lax.fori_loop(0, got_ref.shape[0], place, jnp.zeros((8, LANES), F32))
    spread(
        out_ref,
        product(high_ref, low_ref, weights_ref),
        stacked(jnp.sum(squares, axis=0, keepdims=True)),
    )
    sums_ref[...] = stacked(norm, alpha)


def direction_kernel(got_ref, field_ref, image_ref, sums_ref, keep_ref, norm_ref, send_ref):
    total = jnp.sum(got_ref[...], axis=0)
    norm, alpha, norm_next = sums_ref[0:1], sums_ref[1:2], total[MICS : MICS + 1]
    beta = norm_next / norm
    field, image = wide(field_ref[...]), image_ref[...]
    residual = field - alpha * image
    direction = residual + beta * field
    turned = total[:MICS] + SHIFT * residual + beta * image
    keep_ref[0] = alpha * field
    keep_ref[1] = residual
    keep_ref[2] = direction
    keep_ref[3] = turned
    along = jnp.sum(direction * turned, axis=0, keepdims=True)
    norm_ref[...] = stacked(norm_next)
    send_ref[...] = jnp.broadcast_to(stacked(along)[None], send_ref.shape)


def relay_kernel(got_ref, send_ref):
    total = jnp.sum(got_ref[...], axis=0)
    send_ref[...] = jnp.broadcast_to(total[None], send_ref.shape)


def end_kernel(got_ref, sums_ref, keep_ref, solution_ref, residual_ref):
    frames = solution_ref.shape[1]
    along = jnp.sum(got_ref[:, 0:1, :], axis=0)
    alpha = sums_ref[0:1] / along
    solution_ref[...] = (keep_ref[0] + alpha * keep_ref[2])[:, :frames]
    residual_ref[...] = (keep_ref[1] - alpha * keep_ref[3])[:, :frames]


def call(kernel, outs, **more):
    return pl.pallas_call(
        kernel,
        out_shape=tuple(jax.ShapeDtypeStruct(shape, dtype) for shape, dtype in outs),
        compiler_params=PARAMS,
        **more,
    )


def local(groups, blks, right_side, positions, wavenumber):
    frames = right_side.shape[0]
    field = right_side.T
    rows, cols = blks * MICS, groups * MICS
    block, summed = (MICS, LANES), (MICS + EXTRA, LANES)

    def exchange(value, axis):
        return lax.all_to_all(value, axis, 0, 0)

    scalar = pl.BlockSpec(memory_space=pltpu.SMEM)
    vector = pl.BlockSpec(memory_space=pltpu.VMEM)
    to_cols, to_rows = call(
        start_kernel,
        [((groups,) + block, F32), ((blks,) + block, F32)],
        in_specs=[vector, vector, scalar],
    )(field, positions.T, wavenumber)
    row_blocks = exchange(to_rows, "blk")
    col_blocks = exchange(to_cols, "group")

    partial, high, low = call(
        lambda *refs: first_kernel(frames, *refs),
        [((blks,) + summed, F32), ((rows, cols), BF16), ((rows, cols), BF16)],
        scratch_shapes=[
            pltpu.VMEM((cols, 2 * LANES), BF16),
            pltpu.VMEM((cols, LANES), BF16),
            pltpu.VMEM((rows, LANES), BF16),
        ],
    )(col_blocks, row_blocks, field)
    image, to_cols = call(image_kernel, [(block, F32), ((groups,) + summed, F32)])(
        exchange(partial, "blk"), field
    )
    partial, sums = call(
        lambda *refs: second_kernel(frames, *refs),
        [((blks,) + summed, F32), ((EXTRA, LANES), F32)],
        scratch_shapes=[pltpu.VMEM((cols, 2 * LANES), BF16)],
    )(exchange(to_cols, "group"), col_blocks, high, low)
    keep, norm_next, send = call(
        direction_kernel,
        [((4,) + block, F32), ((EXTRA, LANES), F32), ((blks, EXTRA, LANES), F32)],
    )(exchange(partial, "blk"), field, image, sums)
    (send,) = call(relay_kernel, [((groups, EXTRA, LANES), F32)])(exchange(send, "blk"))
    got = exchange(send, "group")
    solution_field, residual = call(
        end_kernel, [((MICS, frames), F32), ((MICS, frames), F32)]
    )(got, norm_next, keep)
    return solution_field.T, residual.T


def solution(mesh):
    groups, blks = mesh.shape["group"], mesh.shape["blk"]
    where = P(None, ("group", "blk"))
    return jax.shard_map(
        lambda *args: local(groups, blks, *args),
        mesh=mesh,
        in_specs=(where, where, P()),
        out_specs=(where, where),
        check_vma=False,
    )
```

time: 752 us -> 190 us (0.25)
  blocking collectives: 545 us -> 168 us
  waiting for transfers between devices: 139 us -> 0 us
  matrix products: 44.7 us -> 0 us
  Pallas kernels: 0 us -> 18.7 us
  between operations: 14.1 us -> 1.3 us
    psum x3 -> x0, blocking collectives: 295 us -> none  [the longest x2 194 us: squares(): return lax.psum(jnp.sum(vector * vector, axis=1), ('group', 'blk'))]
    all_gather x4 -> x0, blocking collectives: 250 us -> none  [the longest x2 141 us: local(): lax.all_gather(direction, 'group', axis=1, tiled=True)]
    all_to_all x0 -> x7, blocking collectives: none -> 168 us  [exchange(): return lax.all_to_all(value, axis, 0, 0)]
    reduce_scatter x2 -> x0, waiting for transfers between devices: 139 us -> none  [local(): lax.psum_scatter(partial_sum, 'blk', scatter_dimension=1, tiled=True)]
    dot_general x8 -> x0, matrix products: 44.7 us -> none  [one_block(): jnp.dot(dir_part, kernel_block(col_part, rows, kappa), preferred_element_...]
    pallas_call x0 -> x7, Pallas kernels: none -> 18.7 us  [the longest x1 11.1 us: local(): call(lambda *refs: first_kernel(frames, *refs), [((blks,) + summed, F32),...]
  transfers between devices with their start and end apart: 2 -> 0, of which waited for: 2 -> 0; matrix products, arithmetic and copies ran while one was open for 0% -> 0% of each run, Pallas kernels for 0% -> 0%
where the time goes in v1:
time: 190 us
  blocking collectives  168 us (88%)
  Pallas kernels  18.7 us (10%)
    all_to_all x7, blocking collectives, exchange(): return lax.all_to_all(value, axis, 0, 0)  168 us
    pallas_call x1, Pallas kernels, local(): call(lambda *refs: first_kernel(frames, *refs), [((blks,) + summed, F32),...  11.1 us
    pallas_call x1, Pallas kernels, local(): call(lambda *refs: second_kernel(frames, *refs), [((blks,) + summed, F32)...  6.39 us

profile of v1, /device:TPU:1, one launch (start us, length us, event | category | flops | bytes accessed | tf_op | source)
XLA Modules:
  0.0 189.5 jit_solution(7108478825931100209)
XLA Ops:
  1.3 0.8 copy.5
  2.0 0.0 copy-start
  2.1 0.8 copy-done
  2.8 0.4 shard_map.50
  3.2 19.2 %all_to_all.35.refs_1_ = f32[16,64,128]{2,1,0:T(8,128)S(1)} all-to-all(f32[16,64,128]{2,1,0:T(8,128)S(1)} %get-tuple-element.17), channel_id=1, replica_groups=mesh['group'=32,'blk'=16] {'blk'}, dimensions={0} | all-to-all | bytes 1048576 | tf_op jit(solution)/shard_map/all_to_all | solution.py:236
  22.4 37.9 %all_to_all.36.refs_0_.refs_1_ = f32[32,64,128]{2,1,0:T(8,128)S(1)} all-to-all(f32[32,64,128]{2,1,0:T(8,128)S(1)} %get-tuple-element.16), channel_id=1, replica_groups=mesh['group'=32,'blk'=16] {'group'}, dimensions={0} | all-to-all | bytes 2097152 | tf_op jit(solution)/shard_map/all_to_all | solution.py:236
  60.3 11.1 %shard_map.51 = (f32[16,72,128]{2,1,0:T(8,128)S(1)}, bf16[1024,2048]{1,0:T(8,128)(2,1)}, bf16[1024,2048]{1,0:T(8,128)(2,1)}) custom-call(f32[32,64,128]{2,1,0:T(8,128)S(1)} %all_to_all.36.refs_0_.refs_1_, f32[16,64,128]{2,1,0:T(8,128)S(1)} %all_to_all.35.refs_1_, f32[64,96]{1,0:T(8,128)S(1)} %bitcast.5), custom_call_target="tpu_custom_call" | custom-call | tf_op jit(solution)/shard_map/pallas_call | solution.py:248
  71.4 23.0 %all_to_all.37.got_ref = f32[16,72,128]{2,1,0:T(8,128)S(1)} all-to-all(f32[16,72,128]{2,1,0:T(8,128)S(1)} %get-tuple-element.18), channel_id=1, replica_groups=mesh['group'=32,'blk'=16] {'blk'}, dimensions={0} | all-to-all | bytes 1179648 | tf_op jit(solution)/shard_map/all_to_all | solution.py:236
  94.4 0.1 shard_map.52
  94.5 45.7 %all_to_all.38.refs_0_ = f32[32,72,128]{2,1,0:T(8,128)S(1)} all-to-all(f32[32,72,128]{2,1,0:T(8,128)S(1)} %get-tuple-element.19), channel_id=1, replica_groups=mesh['group'=32,'blk'=16] {'group'}, dimensions={0} | all-to-all | bytes 2359296 | tf_op jit(solution)/shard_map/all_to_all | solution.py:236
  140.2 0.0 copy-start.1
  140.2 6.4 %shard_map.53 = (f32[16,72,128]{2,1,0:T(8,128)S(1)}, f32[8,128]{1,0:T(8,128)S(1)}) custom-call(f32[32,72,128]{2,1,0:T(8,128)S(1)} %all_to_all.38.refs_0_, f32[32,64,128]{2,1,0:T(8,128)S(1)} %all_to_all.36.refs_0_.refs_1_, bf16[1024,2048]{1,0:T(8,128)(2,1)} %get-tuple-element.20.refs_2_, bf16[1024,2048]{1,0:T(8,128)(2,1)} %get-tuple-element.21.refs_3_), custom_call_target="tpu_custom_call" | custom-call | tf_op jit(solution)/shard_map/pallas_call | solution.py:260
  146.6 15.1 %all_to_all.39.got_ref = f32[16,72,128]{2,1,0:T(8,128)S(1)} all-to-all(f32[16,72,128]{2,1,0:T(8,128)S(1)} %get-tuple-element.22), channel_id=1, replica_groups=mesh['group'=32,'blk'=16] {'blk'}, dimensions={0} | all-to-all | bytes 1179648 | tf_op jit(solution)/shard_map/all_to_all | solution.py:236
  161.7 0.0 copy-done.1
  161.7 0.1 shard_map.54
  161.7 8.7 %all_to_all.40.got_ref = f32[16,8,128]{2,1,0:T(8,128)S(1)} all-to-all(f32[16,8,128]{2,1,0:T(8,128)S(1)} %get-tuple-element.25), channel_id=1, replica_groups=mesh['group'=32,'blk'=16] {'blk'}, dimensions={0} | all-to-all | bytes 131072 | tf_op jit(solution)/shard_map/all_to_all | solution.py:236
  170.5 18.3 %all_to_all.41.got_ref = f32[32,8,128]{2,1,0:T(8,128)S(1)} all-to-all(f32[32,8,128]{2,1,0:T(8,128)S(1)} %shard_map.55), channel_id=1, replica_groups=mesh['group'=32,'blk'=16] {'group'}, dimensions={0} | all-to-all | bytes 262144 | tf_op jit(solution)/shard_map/all_to_all | solution.py:236
  188.8 0.7 shard_map.56
  (1 shorter events, 0.0 us)
Async XLA Ops:
  2.0 0.8 copy-start
  140.2 21.5 %copy-start.1 = (f32[96,64]{0,1:T(8,128)S(1)}, f32[96,64]{0,1:T(8,128)}, u32[]{:S(2)}) copy-start(f32[96,64]{0,1:T(8,128)} %param.3) | copy-start | bytes 73732

commit v2 on v0

v2 whole, which is shorter than its diff:
```python
import math

import jax
import jax.numpy as jnp
from jax import lax
from jax.experimental import pallas as pl
from jax.experimental.pallas import tpu as pltpu
from jax.sharding import Mesh
from jax.sharding import PartitionSpec as P

LANES = 128
MICS = 64
FRAMES = 96
PACKED = 48
EXTRA = 8
STEP = 256
DEPTH = 64
SHIFT = 0.01
BF16 = jnp.bfloat16
F32 = jnp.float32
AXES = {"z_far": 4, "z_near": 2, "y_far": 4, "y_near": 2, "x": 4, "core": 2}
FAR, FAR_SIZE = ("z_far", "y_far"), 16
NEAR, NEAR_SIZE = ("z_near", "y_near", "x", "core"), 32
ROWS, COLS = NEAR_SIZE * MICS, FAR_SIZE * MICS
SINC = (
    0.9999999403953552,
    -6.579718112945557,
    12.987034797668457,
    -12.193572998046875,
    6.579925060272217,
    -1.9848603010177612,
)
PARAMS = pltpu.CompilerParams(vmem_limit_bytes=48 * 1024 * 1024)


def dot(left, right):
    return lax.dot_general(left, right, (((1,), (0,)), ((), ())), preferred_element_type=F32)


def rounded(value):
    return value.astype(BF16).astype(F32)


def halves(value):
    high = value.astype(BF16)
    return high, (value - high.astype(F32)).astype(BF16)


def widen(value):
    blank = jnp.zeros((value.shape[0], LANES - value.shape[1]), F32)
    return jnp.concatenate([value, blank], axis=1)


def pack(value):
    tail = value[PACKED:]
    third = FRAMES // 3
    spare = [tail[:, i * third : (i + 1) * third] for i in range(3)]
    return jnp.concatenate([value[:PACKED, :FRAMES], jnp.concatenate(spare, axis=0)], axis=1)


def unpack(block):
    spare = block[:, FRAMES:]
    tail = [spare[i * 16 : (i + 1) * 16] for i in range(3)]
    top = widen(block[:, :FRAMES])
    bottom = widen(jnp.concatenate(tail, axis=1))
    return jnp.concatenate([top, bottom], axis=0)


def rows_of(*rows):
    blank = jnp.zeros((EXTRA - len(rows), LANES), F32)
    return jnp.concatenate(list(rows) + [blank], axis=0)


def over_rows(value):
    return jnp.sum(value, axis=0, keepdims=True)


def start_kernel(field_ref, points_ref, col_ref, row_ref):
    points = points_ref[...]
    points = jnp.concatenate([points, jnp.zeros((EXTRA - 3, MICS), F32)], axis=0)
    points = widen(points)
    block = jnp.concatenate([pack(field_ref[...]), points], axis=0)
    col_ref[...] = jnp.broadcast_to(block[None], col_ref.shape)
    row_ref[...] = jnp.broadcast_to(points[None], row_ref.shape)


def factors(points, wave, of_rows):
    scaled = points * (wave * (0.5 / math.pi))
    squares = over_rows(scaled * scaled)

    def thirds(value):
        one = rounded(value)
        two = rounded(value - one)
        return one, two, rounded(value - one - two)

    one, two, three = thirds(scaled)
    ones = jnp.ones_like(squares)
    if of_rows:
        rows = [one, one, two, two, one, three]
        rest = list(thirds(squares)) + [ones] * 3
    else:
        rows = [-2.0 * v for v in (one, two, one, two, three, one)]
        rest = [ones] * 3 + list(thirds(squares))
    blank = jnp.zeros((DEPTH - 6 * EXTRA - 6, squares.shape[1]), F32)
    return jnp.concatenate(rows + rest + [blank], axis=0)


def points_of(ref, count, first):
    tiles = [ref[i, first : first + EXTRA, :MICS] for i in range(count)]
    return jnp.concatenate(tiles, axis=1)


def sinc_of(turns2):
    turns2 = jnp.maximum(turns2, 1e-12)
    inverse = lax.rsqrt(turns2)
    turns = turns2 * inverse
    part = turns - lax.round(turns, lax.RoundingMethod.TO_NEAREST_EVEN)
    square = part * part
    value = SINC[-1] * square + SINC[-2]
    for factor in SINC[-3::-1]:
        value = value * square + factor
    return value * (part * inverse)


def put_weights(weights_ref, index, value):
    at = pl.ds(pl.multiple_of(index * MICS, MICS), MICS)
    high, low = halves(value)
    weights_ref[at, :LANES] = high
    weights_ref[at, LANES:] = low


def send_rows(out_ref, index, both, rest):
    total = both[:, :LANES] + both[:, LANES:] + rest
    for i in range(STEP // MICS):
        packed = pack(total[i * MICS : (i + 1) * MICS])
        out_ref[index * (STEP // MICS) + i, :PACKED, :] = packed


def first_kernel(
    col_ref, row_ref, wave_ref, out_ref, high_ref, low_ref, weights_ref, col_f, row_f
):
    wave = wave_ref[0]

    def place(index, carry):
        put_weights(weights_ref, index, unpack(col_ref[index, :PACKED, :]))
        return carry

    lax.fori_loop(0, FAR_SIZE, place, 0)
    col_f[...] = factors(points_of(col_ref, FAR_SIZE, PACKED), wave, False).astype(BF16)
    row_f[...] = factors(points_of(row_ref, NEAR_SIZE, 0), wave, True).T.astype(BF16)

    def some_rows(index, carry):
        at = pl.ds(pl.multiple_of(index * STEP, STEP), STEP)
        left = row_f[at, :]
        both, rest = jnp.zeros((STEP, 2 * LANES), F32), jnp.zeros((STEP, LANES), F32)
        for first in range(0, COLS, STEP):
            cols = slice(first, first + STEP)
            high, low = halves(sinc_of(dot(left, col_f[:, cols])))
            high_ref[at, cols] = high
            low_ref[at, cols] = low
            both = both + dot(high, weights_ref[cols, :])
            rest = rest + dot(low, weights_ref[cols, :LANES])
        send_rows(out_ref, index, both, rest)
        return carry

    lax.fori_loop(0, ROWS // STEP, some_rows, 0)


def image_kernel(got_ref, field_ref, image_ref, send_ref):
    image = unpack(jnp.sum(got_ref[...], axis=0)) + SHIFT * widen(field_ref[...])
    image_ref[...] = image
    send_ref[...] = jnp.broadcast_to(pack(image)[None], send_ref.shape)


def second_kernel(
    got_ref, col_ref, high_ref, low_ref, out_ref, weights_ref, field_ref, image_ref
):
    def folded(value):
        return jnp.sum(value.reshape(-1, 8, LANES), axis=0)

    def place(index, sums):
        at = pl.ds(pl.multiple_of(index * MICS, MICS), MICS)
        image = unpack(got_ref[index])
        field = unpack(col_ref[index, :PACKED, :])
        put_weights(weights_ref, index, image)
        field_ref[at, :] = field
        image_ref[at, :] = image
        new = (field * field, field * image, image * image)
        return tuple(old + folded(value) for old, value in zip(sums, new))

    blank = jnp.zeros((8, LANES), F32)
    sums = lax.fori_loop(0, FAR_SIZE, place, (blank, blank, blank))
    norm, cross, square = (over_rows(value) for value in sums)
    guess = jnp.where(square > 0.0, cross / jnp.where(square > 0.0, square, 1.0), 0.0)

    def apart(index, sums):
        at = pl.ds(pl.multiple_of(index * MICS, MICS), MICS)
        image = image_ref[at, :]
        left = field_ref[at, :] - guess * image
        return sums[0] + folded(left * left), sums[1] + folded(left * image)

    sums = lax.fori_loop(0, FAR_SIZE, apart, (blank, blank))
    left_norm, left_cross = (over_rows(value) for value in sums)
    extra = rows_of(norm, cross, square, guess, left_norm, left_cross)
    out_ref[:, PACKED:, :] = jnp.broadcast_to(extra[None], (NEAR_SIZE, EXTRA, LANES))

    def some_rows(index, carry):
        at = pl.ds(pl.multiple_of(index * STEP, STEP), STEP)
        both = dot(high_ref[at, :], weights_ref[...])
        rest = dot(low_ref[at, :], weights_ref[:, :LANES])
        send_rows(out_ref, index, both, rest)
        return carry

    lax.fori_loop(0, ROWS // STEP, some_rows, 0)


def direction_kernel(got_ref, field_ref, image_ref, keep_ref, norm_ref, send_ref):
    norm, cross, square, guess, left_norm, left_cross = (
        got_ref[:, PACKED + i, :] for i in range(6)
    )
    norm = over_rows(norm)
    alpha = norm / over_rows(cross)
    off = guess - alpha
    norm_next = over_rows(left_norm + 2.0 * off * left_cross + off * off * square)
    beta = norm_next / norm
    field, image = widen(field_ref[...]), image_ref[...]
    again = unpack(jnp.sum(got_ref[:, :PACKED, :], axis=0)) + SHIFT * image
    residual = field - alpha * image
    direction = residual + beta * field
    turned = image - alpha * again + beta * image
    keep_ref[0] = alpha * field
    keep_ref[1] = residual
    keep_ref[2] = direction
    keep_ref[3] = turned
    norm_ref[...] = rows_of(norm_next)
    along = rows_of(over_rows(direction * turned))
    send_ref[...] = jnp.broadcast_to(along[None], send_ref.shape)


def relay_kernel(got_ref, send_ref):
    total = jnp.sum(got_ref[...], axis=0)
    send_ref[...] = jnp.broadcast_to(total[None], send_ref.shape)


def end_kernel(got_ref, norm_ref, keep_ref, solution_ref, residual_ref):
    along = jnp.sum(got_ref[:, 0:1, :], axis=0)
    alpha = norm_ref[0:1] / along
    solution_ref[...] = (keep_ref[0] + alpha * keep_ref[2])[:, :FRAMES]
    residual_ref[...] = (keep_ref[1] - alpha * keep_ref[3])[:, :FRAMES]


def call(kernel, outs, **more):
    return pl.pallas_call(
        kernel,
        out_shape=tuple(jax.ShapeDtypeStruct(shape, dtype) for shape, dtype in outs),
        compiler_params=PARAMS,
        **more,
    )


def local(right_side, positions, wavenumber):
    field = right_side.T
    block = (MICS, LANES)

    def exchange(value, axis):
        return lax.all_to_all(value, axis, 0, 0)

    scalar = pl.BlockSpec(memory_space=pltpu.SMEM)
    vector = pl.BlockSpec(memory_space=pltpu.VMEM)
    to_cols, to_rows = call(
        start_kernel,
        [((FAR_SIZE, PACKED + EXTRA, LANES), F32), ((NEAR_SIZE, EXTRA, LANES), F32)],
    )(field, positions)
    row_points = exchange(to_rows, NEAR)
    col_blocks = exchange(to_cols, FAR)

    partial, high, low = call(
        first_kernel,
        [((NEAR_SIZE, PACKED, LANES), F32), ((ROWS, COLS), BF16), ((ROWS, COLS), BF16)],
        in_specs=[vector, vector, scalar],
        scratch_shapes=[
            pltpu.VMEM((COLS, 2 * LANES), BF16),
            pltpu.VMEM((DEPTH, COLS), BF16),
            pltpu.VMEM((ROWS, DEPTH), BF16),
        ],
    )(col_blocks, row_points, wavenumber)
    image, to_cols = call(image_kernel, [(block, F32), ((FAR_SIZE, PACKED, LANES), F32)])(
        exchange(partial, NEAR), field
    )
    (partial,) = call(
        second_kernel,
        [((NEAR_SIZE, PACKED + EXTRA, LANES), F32)],
        scratch_shapes=[
            pltpu.VMEM((COLS, 2 * LANES), BF16),
            pltpu.VMEM((COLS, LANES), F32),
            pltpu.VMEM((COLS, LANES), F32),
        ],
    )(exchange(to_cols, FAR), col_blocks, high, low)
    keep, norm_next, send = call(
        direction_kernel,
        [((4,) + block, F32), ((EXTRA, LANES), F32), ((NEAR_SIZE, EXTRA, LANES), F32)],
    )(exchange(partial, NEAR), field, image)
    (send,) = call(relay_kernel, [((FAR_SIZE, EXTRA, LANES), F32)])(exchange(send, NEAR))
    solution_field, residual = call(
        end_kernel, [((MICS, FRAMES), F32), ((MICS, FRAMES), F32)]
    )(exchange(send, FAR), norm_next, keep)
    return solution_field.T, residual.T


def solution(mesh):
    fine = Mesh(mesh.devices.reshape(tuple(AXES.values())), tuple(AXES))
    where = P(None, tuple(AXES))
    return jax.shard_map(
        local,
        mesh=fine,
        in_specs=(where, where, P()),
        out_specs=(where, where),
        check_vma=False,
    )
```

time: 752 us -> 162 us (0.22)
  blocking collectives: 545 us -> 104 us
  waiting for transfers between devices: 139 us -> 16.3 us
  matrix products: 44.7 us -> 0 us
  Pallas kernels: 0 us -> 25.2 us
  between operations: 14.1 us -> 1.31 us
  starting transfers between devices: 0.08 us -> 12.6 us
    psum x3 -> x0, blocking collectives: 295 us -> none  [the longest x2 194 us: squares(): return lax.psum(jnp.sum(vector * vector, axis=1), ('group', 'blk'))]
    all_gather x4 -> x0, blocking collectives: 250 us -> none  [the longest x2 141 us: local(): lax.all_gather(direction, 'group', axis=1, tiled=True)]
    reduce_scatter x2 -> x0, waiting for transfers between devices: 139 us -> none  [local(): lax.psum_scatter(partial_sum, 'blk', scatter_dimension=1, tiled=True)]
    all_to_all x0 -> x6, blocking collectives: none -> 104 us  [exchange(): return lax.all_to_all(value, axis, 0, 0)]
    dot_general x8 -> x0, matrix products: 44.7 us -> none  [one_block(): jnp.dot(dir_part, kernel_block(col_part, rows, kappa), preferred_element_...]
    pallas_call x0 -> x7, Pallas kernels: none -> 25.2 us  [the longest x1 14.8 us: local(): call(first_kernel, [((NEAR_SIZE, PACKED, LANES), F32), ((ROWS, COLS), BF1...]
    all_to_all x0 -> x1, waiting for transfers between devices: none -> 16.3 us  [exchange(): return lax.all_to_all(value, axis, 0, 0)]
    all_to_all x0 -> x1, starting transfers between devices: none -> 12.6 us  [exchange(): return lax.all_to_all(value, axis, 0, 0)]
  transfers between devices with their start and end apart: 2 -> 1, of which waited for: 2 -> 1; matrix products, arithmetic and copies ran while one was open for 0% -> 0% of each run, Pallas kernels for 0% -> 0%
where the time goes in v2:
time: 162 us; the launch traced here: 161 us
  blocking collectives  104 us (64%)
  Pallas kernels  25.2 us (16%)
  waiting for transfers between devices  16.3 us (10%)
  starting transfers between devices  12.6 us (8%)
  local copies, waits for them, and re-layouts  2.19 us (1%)
    all_to_all x6, blocking collectives, exchange(): return lax.all_to_all(value, axis, 0, 0)  104 us
    all_to_all x1, waiting for transfers between devices, exchange(): return lax.all_to_all(value, axis, 0, 0)  16.3 us
    pallas_call x1, Pallas kernels, local(): call(first_kernel, [((NEAR_SIZE, PACKED, LANES), F32), ((ROWS, COLS), BF1...  14.8 us
    all_to_all x1, starting transfers between devices, exchange(): return lax.all_to_all(value, axis, 0, 0)  12.6 us
    pallas_call x1, Pallas kernels, local(): call(second_kernel, [((NEAR_SIZE, PACKED + EXTRA, LANES), F32)], scratch_...  8.38 us
  transfers between devices with their start and end apart: 1, of which 1 were waited for; matrix products, arithmetic and copies ran while one was open for 0% of the time, Pallas kernels for 0%

profile of v2, /device:TPU:1, one launch (start us, length us, event | category | flops | bytes accessed | tf_op | source)
XLA Modules:
  0.0 161.4 jit_solution(6281756668316268884)
XLA Ops:
  0.6 0.0 copy-start
  0.6 0.7 copy-done
  1.4 0.0 copy-start.2
  1.4 0.7 copy-done.2
  2.1 0.9 shard_map.50
  3.0 16.7 %all_to_all.35.row_ref = f32[32,8,128]{2,1,0:T(8,128)S(1)} all-to-all(f32[32,8,128]{2,1,0:T(8,128)S(1)} %get-tuple-element.15), channel_id=1, replica_groups=mesh['z_far'=4,'z_near'=2,'y_far'=4,'y_near'=2,'x'=4,'core'=2] {'z_near'..., dimensions={0} | all-to-all | bytes 262144 | tf_op jit(solution)/shard_map/all_to_all | solution.py:266
  19.7 12.6 %all-to-all-start = ((f32[16,56,128]{2,1,0:T(8,128)}), f32[16,56,128]{2,1,0:T(8,128)S(1)}, u32[]{:S(2)}, u32[]{:S(2)}) async-start(f32[16,56,128]{2,1,0:T(8,128)} %get-tuple-element.14), calls=%async_computation | async-start | bytes 917504 | tf_op jit(solution)/shard_map/all_to_all | solution.py:266
  32.9 16.3 %all-to-all-done.col_ref = f32[16,56,128]{2,1,0:T(8,128)S(1)} async-done(((f32[16,56,128]{2,1,0:T(8,128)}), f32[16,56,128]{2,1,0:T(8,128)S(1)}, u32[]{:S(2)}, u32[]{:S(2)}) %all-to-all-start) | async-done | bytes 458784 | tf_op jit(solution)/shard_map/all_to_all | solution.py:266
  49.2 14.8 %shard_map.51 = (f32[32,48,128]{2,1,0:T(8,128)S(1)}, bf16[2048,1024]{1,0:T(8,128)(2,1)S(1)}, bf16[2048,1024]{1,0:T(8,128)(2,1)}) custom-call(f32[16,56,128]{2,1,0:T(8,128)S(1)} %all-to-all-done.col_ref, f32[32,8,128]{2,1,0:T(8,128)S(1)} %all_to_all.35.row_ref, f32[1]{0:T(128)S(6)} %copy.5.wave_ref), custom_call_target="tpu_custom_call" | custom-call | tf_op jit(solution)/shard_map/pallas_call | solution.py:277
  64.0 19.0 %all_to_all.36.got_ref = f32[32,48,128]{2,1,0:T(8,128)S(1)} all-to-all(f32[32,48,128]{2,1,0:T(8,128)S(1)} %get-tuple-element.16), channel_id=1, replica_groups=mesh['z_far'=4,'z_near'=2,'y_far'=4,'y_near'=2,'x'=4,'core'=2] {'z_near'..., dimensions={0} | all-to-all | bytes 1572864 | tf_op jit(solution)/shard_map/all_to_all | solution.py:266
  83.0 0.0 copy-start.1
  83.0 0.8 copy-done.1
  83.8 0.3 shard_map.52
  84.1 21.4 %all_to_all.37.got_ref = f32[16,48,128]{2,1,0:T(8,128)S(1)} all-to-all(f32[16,48,128]{2,1,0:T(8,128)S(1)} %get-tuple-element.17), channel_id=1, replica_groups=mesh['z_far'=4,'z_near'=2,'y_far'=4,'y_near'=2,'x'=4,'core'=2] {'z_far',..., dimensions={0} | all-to-all | bytes 786432 | tf_op jit(solution)/shard_map/all_to_all | solution.py:266
  105.5 8.4 %shard_map.53 = f32[32,56,128]{2,1,0:T(8,128)S(1)} custom-call(f32[16,48,128]{2,1,0:T(8,128)S(1)} %all_to_all.37.got_ref, f32[16,56,128]{2,1,0:T(8,128)S(1)} %all-to-all-done.col_ref, bf16[2048,1024]{1,0:T(8,128)(2,1)S(1)} %get-tuple-element.18.high_ref, bf16[2048,1024]{1,0:T(8,128)(2,1)} %get-tuple-element.19.low_ref), custom_call_target="tpu_custom_call" | custom-call | tf_op jit(solution)/shard_map/pallas_call | solution.py:290
  113.9 20.1 %all_to_all.38.got_ref = f32[32,56,128]{2,1,0:T(8,128)S(1)} all-to-all(f32[32,56,128]{2,1,0:T(8,128)S(1)} %shard_map.53), channel_id=1, replica_groups=mesh['z_far'=4,'z_near'=2,'y_far'=4,'y_near'=2,'x'=4,'core'=2] {'z_near'..., dimensions={0} | all-to-all | bytes 1835008 | tf_op jit(solution)/shard_map/all_to_all | solution.py:266
  134.0 0.2 shard_map.54
  134.2 10.3 %all_to_all.39.got_ref = f32[32,8,128]{2,1,0:T(8,128)S(1)} all-to-all(f32[32,8,128]{2,1,0:T(8,128)S(1)} %get-tuple-element.21), channel_id=1, replica_groups=mesh['z_far'=4,'z_near'=2,'y_far'=4,'y_near'=2,'x'=4,'core'=2] {'z_near'..., dimensions={0} | all-to-all | bytes 262144 | tf_op jit(solution)/shard_map/all_to_all | solution.py:266
  144.5 16.2 %all_to_all.40.got_ref = f32[16,8,128]{2,1,0:T(8,128)S(1)} all-to-all(f32[16,8,128]{2,1,0:T(8,128)S(1)} %shard_map.55), channel_id=1, replica_groups=mesh['z_far'=4,'z_near'=2,'y_far'=4,'y_near'=2,'x'=4,'core'=2] {'z_far',..., dimensions={0} | all-to-all | bytes 131072 | tf_op jit(solution)/shard_map/all_to_all | solution.py:266
  160.7 0.7 shard_map.56
  (1 shorter events, 0.0 us)
Async XLA Ops:
  0.6 0.8 copy-start
  1.4 0.7 copy-start.2
  19.7 29.5 %all-to-all-start = ((f32[16,56,128]{2,1,0:T(8,128)}), f32[16,56,128]{2,1,0:T(8,128)S(1)}, u32[]{:S(2)}, u32[]{:S(2)}) async-start(f32[16,56,128]{2,1,0:T(8,128)} %get-tuple-element.14), calls=%async_computation | async-start | bytes 917504 | tf_op jit(solution)/shard_map/all_to_all | solution.py:266
  83.0 0.8 copy-start.1

commit v3 on v2

--- a/solution.py
+++ b/solution.py
@@ -30,7 +30,7 @@
     6.579925060272217,
     -1.9848603010177612,
 )
-PARAMS = pltpu.CompilerParams(vmem_limit_bytes=48 * 1024 * 1024)
+PARAMS = pltpu.CompilerParams(vmem_limit_bytes=24 * 1024 * 1024)
 
 
 def dot(left, right):
@@ -129,7 +129,10 @@
     weights_ref[at, LANES:] = low
 
 
-def send_rows(out_ref, index, both, rest):
+def send_rows(out_ref, index, high_ref, low_ref, weights_ref):
+    at = pl.ds(pl.multiple_of(index * STEP, STEP), STEP)
+    both = dot(high_ref[at, :], weights_ref[...])
+    rest = dot(low_ref[at, :], weights_ref[:, :LANES])
     total = both[:, :LANES] + both[:, LANES:] + rest
     for i in range(STEP // MICS):
         packed = pack(total[i * MICS : (i + 1) * MICS])
@@ -145,25 +148,22 @@
         put_weights(weights_ref, index, unpack(col_ref[index, :PACKED, :]))
         return carry
 
-    lax.fori_loop(0, FAR_SIZE, place, 0)
+    lax.fori_loop(0, FAR_SIZE, place, 0, unroll=True)
     col_f[...] = factors(points_of(col_ref, FAR_SIZE, PACKED), wave, False).astype(BF16)
     row_f[...] = factors(points_of(row_ref, NEAR_SIZE, 0), wave, True).T.astype(BF16)
 
     def some_rows(index, carry):
         at = pl.ds(pl.multiple_of(index * STEP, STEP), STEP)
         left = row_f[at, :]
-        both, rest = jnp.zeros((STEP, 2 * LANES), F32), jnp.zeros((STEP, LANES), F32)
         for first in range(0, COLS, STEP):
             cols = slice(first, first + STEP)
             high, low = halves(sinc_of(dot(left, col_f[:, cols])))
             high_ref[at, cols] = high
             low_ref[at, cols] = low
-            both = both + dot(high, weights_ref[cols, :])
-            rest = rest + dot(low, weights_ref[cols, :LANES])
-        send_rows(out_ref, index, both, rest)
+        send_rows(out_ref, index, high_ref, low_ref, weights_ref)
         return carry
 
-    lax.fori_loop(0, ROWS // STEP, some_rows, 0)
+    lax.fori_loop(0, ROWS // STEP, some_rows, 0, unroll=True)
 
 
 def image_kernel(got_ref, field_ref, image_ref, send_ref):
@@ -189,7 +189,7 @@
         return tuple(old + folded(value) for old, value in zip(sums, new))
 
     blank = jnp.zeros((8, LANES), F32)
-    sums = lax.fori_loop(0, FAR_SIZE, place, (blank, blank, blank))
+    sums = lax.fori_loop(0, FAR_SIZE, place, (blank, blank, blank), unroll=True)
     norm, cross, square = (over_rows(value) for value in sums)
     guess = jnp.where(square > 0.0, cross / jnp.where(square > 0.0, square, 1.0), 0.0)
 
@@ -199,19 +199,16 @@
         left = field_ref[at, :] - guess * image
         return sums[0] + folded(left * left), sums[1] + folded(left * image)
 
-    sums = lax.fori_loop(0, FAR_SIZE, apart, (blank, blank))
+    sums = lax.fori_loop(0, FAR_SIZE, apart, (blank, blank), unroll=True)
     left_norm, left_cross = (over_rows(value) for value in sums)
     extra = rows_of(norm, cross, square, guess, left_norm, left_cross)
     out_ref[:, PACKED:, :] = jnp.broadcast_to(extra[None], (NEAR_SIZE, EXTRA, LANES))
 
     def some_rows(index, carry):
-        at = pl.ds(pl.multiple_of(index * STEP, STEP), STEP)
-        both = dot(high_ref[at, :], weights_ref[...])
-        rest = dot(low_ref[at, :], weights_ref[:, :LANES])
-        send_rows(out_ref, index, both, rest)
+        send_rows(out_ref, index, high_ref, low_ref, weights_ref)
         return carry
 
-    lax.fori_loop(0, ROWS // STEP, some_rows, 0)
+    lax.fori_loop(0, ROWS // STEP, some_rows, 0, unroll=True)
 
 
 def direction_kernel(got_ref, field_ref, image_ref, keep_ref, norm_ref, send_ref):

time: 162 us -> 151 us (0.932)
  Pallas kernels: 25.2 us -> 13.8 us
    pallas_call x1, Pallas kernels: 14.8 us -> 9.03 us  [local(): call(first_kernel, [((NEAR_SIZE, PACKED, LANES), F32), ((ROWS, COLS), BF1...]
    pallas_call x1, Pallas kernels: 8.38 us -> 2.72 us  [local(): call(second_kernel, [((NEAR_SIZE, PACKED + EXTRA, LANES), F32)], scratch_...]
where the time goes in v3:
time: 151 us; the launch traced here: 150 us
  blocking collectives  104 us (69%)
  waiting for transfers between devices  16.3 us (11%)
  Pallas kernels  13.8 us (9%)
  starting transfers between devices  12.6 us (8%)
  local copies, waits for them, and re-layouts  2.2 us (1%)
    all_to_all x6, blocking collectives, exchange(): return lax.all_to_all(value, axis, 0, 0)  104 us
    all_to_all x1, waiting for transfers between devices, exchange(): return lax.all_to_all(value, axis, 0, 0)  16.3 us
    all_to_all x1, starting transfers between devices, exchange(): return lax.all_to_all(value, axis, 0, 0)  12.6 us
    pallas_call x1, Pallas kernels, local(): call(first_kernel, [((NEAR_SIZE, PACKED, LANES), F32), ((ROWS, COLS), BF1...  9.03 us
  transfers between devices with their start and end apart: 1, of which 1 were waited for; matrix products, arithmetic and copies ran while one was open for 0% of the time, Pallas kernels for 0%

profile of v3, /device:TPU:1, one launch (start us, length us, event | category | flops | bytes accessed | tf_op | source)
XLA Modules:
  0.0 150.0 jit_solution(16998088417631618298)
XLA Ops:
  0.6 0.0 copy-start
  0.6 0.7 copy-done
  1.4 0.0 copy-start.3
  1.4 0.7 copy-done.3
  2.1 0.9 shard_map.50
  3.0 16.7 %all_to_all.35.row_ref = f32[32,8,128]{2,1,0:T(8,128)S(1)} all-to-all(f32[32,8,128]{2,1,0:T(8,128)S(1)} %get-tuple-element.15), channel_id=1, replica_groups=mesh['z_far'=4,'z_near'=2,'y_far'=4,'y_near'=2,'x'=4,'core'=2] {'z_near'..., dimensions={0} | all-to-all | bytes 262144 | tf_op jit(solution)/shard_map/all_to_all | solution.py:263
  19.7 12.6 %all-to-all-start = ((f32[16,56,128]{2,1,0:T(8,128)}), f32[16,56,128]{2,1,0:T(8,128)S(1)}, u32[]{:S(2)}, u32[]{:S(2)}) async-start(f32[16,56,128]{2,1,0:T(8,128)} %get-tuple-element.14), calls=%async_computation | async-start | bytes 917504 | tf_op jit(solution)/shard_map/all_to_all | solution.py:263
  32.9 16.3 %all-to-all-done.col_ref = f32[16,56,128]{2,1,0:T(8,128)S(1)} async-done(((f32[16,56,128]{2,1,0:T(8,128)}), f32[16,56,128]{2,1,0:T(8,128)S(1)}, u32[]{:S(2)}, u32[]{:S(2)}) %all-to-all-start) | async-done | bytes 458784 | tf_op jit(solution)/shard_map/all_to_all | solution.py:263
  49.2 9.0 %shard_map.51 = (f32[32,48,128]{2,1,0:T(8,128)S(1)}, bf16[2048,1024]{1,0:T(8,128)(2,1)S(1)}, bf16[2048,1024]{1,0:T(8,128)(2,1)S(1)}) custom-call(f32[16,56,128]{2,1,0:T(8,128)S(1)} %all-to-all-done.col_ref, f32[32,8,128]{2,1,0:T(8,128)S(1)} %all_to_all.35.row_ref, f32[1]{0:T(128)S(6)} %copy.5.wave_ref), custom_call_target="tpu_custom_call" | custom-call | tf_op jit(solution)/shard_map/pallas_call | solution.py:274
  58.2 19.0 %all_to_all.36.got_ref = f32[32,48,128]{2,1,0:T(8,128)S(1)} all-to-all(f32[32,48,128]{2,1,0:T(8,128)S(1)} %get-tuple-element.16), channel_id=1, replica_groups=mesh['z_far'=4,'z_near'=2,'y_far'=4,'y_near'=2,'x'=4,'core'=2] {'z_near'..., dimensions={0} | all-to-all | bytes 1572864 | tf_op jit(solution)/shard_map/all_to_all | solution.py:263
  77.3 0.0 copy-start.1
  77.3 0.8 copy-done.1
  78.1 0.3 shard_map.52
  78.3 21.4 %all_to_all.37.got_ref = f32[16,48,128]{2,1,0:T(8,128)S(1)} all-to-all(f32[16,48,128]{2,1,0:T(8,128)S(1)} %get-tuple-element.17), channel_id=1, replica_groups=mesh['z_far'=4,'z_near'=2,'y_far'=4,'y_near'=2,'x'=4,'core'=2] {'z_far',..., dimensions={0} | all-to-all | bytes 786432 | tf_op jit(solution)/shard_map/all_to_all | solution.py:263
  99.8 0.0 copy-start.2
  99.8 2.7 %shard_map.53 = f32[32,56,128]{2,1,0:T(8,128)S(1)} custom-call(f32[16,48,128]{2,1,0:T(8,128)S(1)} %all_to_all.37.got_ref, f32[16,56,128]{2,1,0:T(8,128)S(1)} %all-to-all-done.col_ref, bf16[2048,1024]{1,0:T(8,128)(2,1)S(1)} %get-tuple-element.18.high_ref, bf16[2048,1024]{1,0:T(8,128)(2,1)S(1)} %get-tuple-element.19.low_ref), custom_call_target="tpu_custom_call" | custom-call | tf_op jit(solution)/shard_map/pallas_call | solution.py:287
  102.5 20.1 %all_to_all.38.got_ref = f32[32,56,128]{2,1,0:T(8,128)S(1)} all-to-all(f32[32,56,128]{2,1,0:T(8,128)S(1)} %shard_map.53), channel_id=1, replica_groups=mesh['z_far'=4,'z_near'=2,'y_far'=4,'y_near'=2,'x'=4,'core'=2] {'z_near'..., dimensions={0} | all-to-all | bytes 1835008 | tf_op jit(solution)/shard_map/all_to_all | solution.py:263
  122.6 0.0 copy-done.2
  122.6 0.2 shard_map.54
  122.8 10.3 %all_to_all.39.got_ref = f32[32,8,128]{2,1,0:T(8,128)S(1)} all-to-all(f32[32,8,128]{2,1,0:T(8,128)S(1)} %get-tuple-element.21), channel_id=1, replica_groups=mesh['z_far'=4,'z_near'=2,'y_far'=4,'y_near'=2,'x'=4,'core'=2] {'z_near'..., dimensions={0} | all-to-all | bytes 262144 | tf_op jit(solution)/shard_map/all_to_all | solution.py:263
  133.1 16.2 %all_to_all.40.got_ref = f32[16,8,128]{2,1,0:T(8,128)S(1)} all-to-all(f32[16,8,128]{2,1,0:T(8,128)S(1)} %shard_map.55), channel_id=1, replica_groups=mesh['z_far'=4,'z_near'=2,'y_far'=4,'y_near'=2,'x'=4,'core'=2] {'z_far',..., dimensions={0} | all-to-all | bytes 131072 | tf_op jit(solution)/shard_map/all_to_all | solution.py:263
  149.3 0.7 shard_map.56
  (1 shorter events, 0.0 us)
Async XLA Ops:
  0.6 0.8 copy-start
  1.4 0.7 copy-start.3
  19.7 29.5 %all-to-all-start = ((f32[16,56,128]{2,1,0:T(8,128)}), f32[16,56,128]{2,1,0:T(8,128)S(1)}, u32[]{:S(2)}, u32[]{:S(2)}) async-start(f32[16,56,128]{2,1,0:T(8,128)} %get-tuple-element.14), calls=%async_computation | async-start | bytes 917504 | tf_op jit(solution)/shard_map/all_to_all | solution.py:263
  77.3 0.8 copy-start.1
  99.8 22.9 %copy-start.2 = (f32[96,64]{0,1:T(8,128)S(1)}, f32[96,64]{0,1:T(8,128)}, u32[]{:S(2)}) copy-start(f32[96,64]{0,1:T(8,128)} %param.3) | copy-start | bytes 73732

commit v4 on v3

--- a/solution.py
+++ b/solution.py
@@ -20,8 +20,10 @@
 F32 = jnp.float32
 AXES = {"z_far": 4, "z_near": 2, "y_far": 4, "y_near": 2, "x": 4, "core": 2}
 FAR, FAR_SIZE = ("z_far", "y_far"), 16
-NEAR, NEAR_SIZE = ("z_near", "y_near", "x", "core"), 32
-ROWS, COLS = NEAR_SIZE * MICS, FAR_SIZE * MICS
+MID, MID_SIZE = ("z_near", "y_near", "x"), 16
+NEAR, NEAR_SIZE = MID + ("core",), 32
+GATHERED = 2 * FAR_SIZE
+ROWS, COLS = MID_SIZE * MICS, GATHERED * MICS
 SINC = (
     0.9999999403953552,
     -6.579718112945557,
@@ -148,9 +150,9 @@
         put_weights(weights_ref, index, unpack(col_ref[index, :PACKED, :]))
         return carry
 
-    lax.fori_loop(0, FAR_SIZE, place, 0, unroll=True)
-    col_f[...] = factors(points_of(col_ref, FAR_SIZE, PACKED), wave, False).astype(BF16)
-    row_f[...] = factors(points_of(row_ref, NEAR_SIZE, 0), wave, True).T.astype(BF16)
+    lax.fori_loop(0, GATHERED, place, 0, unroll=True)
+    col_f[...] = factors(points_of(col_ref, GATHERED, PACKED), wave, False).astype(BF16)
+    row_f[...] = factors(points_of(row_ref, MID_SIZE, 0), wave, True).T.astype(BF16)
 
     def some_rows(index, carry):
         at = pl.ds(pl.multiple_of(index * STEP, STEP), STEP)
@@ -189,7 +191,7 @@
         return tuple(old + folded(value) for old, value in zip(sums, new))
 
     blank = jnp.zeros((8, LANES), F32)
-    sums = lax.fori_loop(0, FAR_SIZE, place, (blank, blank, blank), unroll=True)
+    sums = lax.fori_loop(0, GATHERED, place, (blank, blank, blank), unroll=True)
     norm, cross, square = (over_rows(value) for value in sums)
     guess = jnp.where(square > 0.0, cross / jnp.where(square > 0.0, square, 1.0), 0.0)
 
@@ -199,10 +201,10 @@
         left = field_ref[at, :] - guess * image
         return sums[0] + folded(left * left), sums[1] + folded(left * image)
 
-    sums = lax.fori_loop(0, FAR_SIZE, apart, (blank, blank), unroll=True)
+    sums = lax.fori_loop(0, GATHERED, apart, (blank, blank), unroll=True)
     left_norm, left_cross = (over_rows(value) for value in sums)
     extra = rows_of(norm, cross, square, guess, left_norm, left_cross)
-    out_ref[:, PACKED:, :] = jnp.broadcast_to(extra[None], (NEAR_SIZE, EXTRA, LANES))
+    out_ref[:, PACKED:, :] = jnp.broadcast_to(extra[None], (MID_SIZE, EXTRA, LANES))
 
     def some_rows(index, carry):
         send_rows(out_ref, index, high_ref, low_ref, weights_ref)
@@ -262,18 +264,22 @@
     def exchange(value, axis):
         return lax.all_to_all(value, axis, 0, 0)
 
+    def gather(value):
+        both = lax.all_gather(exchange(value, FAR), "core")
+        return both.reshape((GATHERED,) + value.shape[1:])
+
     scalar = pl.BlockSpec(memory_space=pltpu.SMEM)
     vector = pl.BlockSpec(memory_space=pltpu.VMEM)
-    to_cols, to_rows = call(
+    to_cols, points = call(
         start_kernel,
-        [((FAR_SIZE, PACKED + EXTRA, LANES), F32), ((NEAR_SIZE, EXTRA, LANES), F32)],
+        [((FAR_SIZE, PACKED + EXTRA, LANES), F32), ((MID_SIZE, EXTRA, LANES), F32)],
     )(field, positions)
-    row_points = exchange(to_rows, NEAR)
-    col_blocks = exchange(to_cols, FAR)
+    col_blocks = gather(to_cols)
+    row_points = exchange(points, MID)
 
     partial, high, low = call(
         first_kernel,
-        [((NEAR_SIZE, PACKED, LANES), F32), ((ROWS, COLS), BF16), ((ROWS, COLS), BF16)],
+        [((MID_SIZE, PACKED, LANES), F32), ((ROWS, COLS), BF16), ((ROWS, COLS), BF16)],
         in_specs=[vector, vector, scalar],
         scratch_shapes=[
             pltpu.VMEM((COLS, 2 * LANES), BF16),
@@ -282,21 +288,21 @@
         ],
     )(col_blocks, row_points, wavenumber)
     image, to_cols = call(image_kernel, [(block, F32), ((FAR_SIZE, PACKED, LANES), F32)])(
-        exchange(partial, NEAR), field
+        exchange(partial, MID), field
     )
     (partial,) = call(
         second_kernel,
-        [((NEAR_SIZE, PACKED + EXTRA, LANES), F32)],
+        [((MID_SIZE, PACKED + EXTRA, LANES), F32)],
         scratch_shapes=[
             pltpu.VMEM((COLS, 2 * LANES), BF16),
             pltpu.VMEM((COLS, LANES), F32),
             pltpu.VMEM((COLS, LANES), F32),
         ],
-    )(exchange(to_cols, FAR), col_blocks, high, low)
+    )(gather(to_cols), col_blocks, high, low)
     keep, norm_next, send = call(
         direction_kernel,
         [((4,) + block, F32), ((EXTRA, LANES), F32), ((NEAR_SIZE, EXTRA, LANES), F32)],
-    )(exchange(partial, NEAR), field, image)
+    )(exchange(partial, MID), field, image)
     (send,) = call(relay_kernel, [((FAR_SIZE, EXTRA, LANES), F32)])(exchange(send, NEAR))
     solution_field, residual = call(
         end_kernel, [((MICS, FRAMES), F32), ((MICS, FRAMES), F32)]

time: 151 us -> 139 us (0.921)
  blocking collectives: 104 us -> 82.1 us
  starting transfers between devices: 12.6 us -> 21.2 us
  waiting for transfers between devices: 16.3 us -> 18 us
    all_to_all x6 -> x5, blocking collectives: 104 us -> 71.3 us  [exchange(): return lax.all_to_all(value, axis, 0, 0)]
    all_gather x0 -> x2, blocking collectives: none -> 10.8 us  [gather(): both = lax.all_gather(exchange(value, FAR), 'core')]
    all_to_all x1 -> x2, starting transfers between devices: 12.6 us -> 21.2 us  [exchange(): return lax.all_to_all(value, axis, 0, 0)]
    all_to_all x1 -> x2, waiting for transfers between devices: 16.3 us -> 18 us  [exchange(): return lax.all_to_all(value, axis, 0, 0)]
  transfers between devices with their start and end apart: 1 -> 2, of which waited for: 1 -> 2; matrix products, arithmetic and copies ran while one was open for 0% -> 0% of each run, Pallas kernels for 0% -> 0%
where the time goes in v4:
time: 139 us; the launch traced here: 138 us
  blocking collectives  82.1 us (59%)
  starting transfers between devices  21.2 us (15%)
  waiting for transfers between devices  18 us (13%)
  Pallas kernels  13.9 us (10%)
  local copies, waits for them, and re-layouts  1.44 us (1%)
    all_to_all x5, blocking collectives, exchange(): return lax.all_to_all(value, axis, 0, 0)  71.3 us
    all_to_all x2, starting transfers between devices, exchange(): return lax.all_to_all(value, axis, 0, 0)  21.2 us
    all_to_all x2, waiting for transfers between devices, exchange(): return lax.all_to_all(value, axis, 0, 0)  18 us
    all_gather x2, blocking collectives, gather(): both = lax.all_gather(exchange(value, FAR), 'core')  10.8 us
    pallas_call x1, Pallas kernels, local(): call(first_kernel, [((MID_SIZE, PACKED, LANES), F32), ((ROWS, COLS), BF16...  8.94 us
    pallas_call x1, Pallas kernels, local(): call(second_kernel, [((MID_SIZE, PACKED + EXTRA, LANES), F32)], scratch_s...  2.92 us
  transfers between devices with their start and end apart: 2, of which 2 were waited for; matrix products, arithmetic and copies ran while one was open for 0% of the time, Pallas kernels for 0%

profile of v4, /device:TPU:1, one launch (start us, length us, event | category | flops | bytes accessed | tf_op | source)
XLA Modules:
  0.0 138.0 jit_solution(13329780019852444058)
XLA Ops:
  0.6 0.0 copy-start
  0.6 0.7 copy-done
  1.4 0.0 copy-start.2
  1.4 0.7 copy-done.2
  2.1 0.0 copy-start.1
  2.1 0.9 shard_map.50
  3.0 16.2 %all-to-all-start = ((f32[16,56,128]{2,1,0:T(8,128)}), f32[16,56,128]{2,1,0:T(8,128)S(1)}, u32[]{:S(2)}, u32[]{:S(2)}) async-start(f32[16,56,128]{2,1,0:T(8,128)} %get-tuple-element.14), calls=%async_computation | async-start | bytes 917504 | tf_op jit(solution)/shard_map/all_to_all | solution.py:265
  19.9 16.4 %all-to-all-done = f32[16,56,128]{2,1,0:T(8,128)S(1)} async-done(((f32[16,56,128]{2,1,0:T(8,128)}), f32[16,56,128]{2,1,0:T(8,128)S(1)}, u32[]{:S(2)}, u32[]{:S(2)}) %all-to-all-start) | async-done | bytes 458784 | tf_op jit(solution)/shard_map/all_to_all | solution.py:265
  36.3 5.0 %all-to-all-start.1 = ((f32[16,8,128]{2,1,0:T(8,128)}), f32[16,8,128]{2,1,0:T(8,128)S(1)}, u32[]{:S(2)}, u32[]{:S(2)}) async-start(f32[16,8,128]{2,1,0:T(8,128)} %get-tuple-element.15), calls=%async_computation.1 | async-start | bytes 131072 | tf_op jit(solution)/shard_map/all_to_all | solution.py:265
  41.4 4.7 %all-gather.col_ref = f32[32,56,128]{2,1,0:T(8,128)S(1)} all-gather(f32[16,56,128]{2,1,0:T(8,128)S(1)} %all-to-all-done), channel_id=2, replica_groups=mesh['z_far'=4,'z_near'=2,'y_far'=4,'y_near'=2,'x'=4,'core'=2] {'core'}, dimensions={0}, use_global_device_ids=true | all-gather | bytes 1376256 | tf_op jit(solution)/shard_map/all_gather | solution.py:268
  46.0 1.5 %all-to-all-done.1.row_ref = f32[16,8,128]{2,1,0:T(8,128)S(1)} async-done(((f32[16,8,128]{2,1,0:T(8,128)}), f32[16,8,128]{2,1,0:T(8,128)S(1)}, u32[]{:S(2)}, u32[]{:S(2)}) %all-to-all-start.1) | async-done | bytes 65568 | tf_op jit(solution)/shard_map/all_to_all | solution.py:265
  47.5 8.9 %shard_map.51 = (f32[16,48,128]{2,1,0:T(8,128)S(1)}, bf16[1024,2048]{1,0:T(8,128)(2,1)S(1)}, bf16[1024,2048]{1,0:T(8,128)(2,1)S(1)}) custom-call(f32[32,56,128]{2,1,0:T(8,128)S(1)} %all-gather.col_ref, f32[16,8,128]{2,1,0:T(8,128)S(1)} %all-to-all-done.1.row_ref, f32[1]{0:T(128)S(6)} %copy.5.wave_ref), custom_call_target="tpu_custom_call" | custom-call | tf_op jit(solution)/shard_map/pallas_call | solution.py:280
  56.5 12.7 %all_to_all.35.got_ref = f32[16,48,128]{2,1,0:T(8,128)S(1)} all-to-all(f32[16,48,128]{2,1,0:T(8,128)S(1)} %get-tuple-element.16), channel_id=1, replica_groups=mesh['z_far'=4,'z_near'=2,'y_far'=4,'y_near'=2,'x'=4,'core'=2] {'z_near'..., dimensions={0} | all-to-all | bytes 786432 | tf_op jit(solution)/shard_map/all_to_all | solution.py:265
  69.2 0.0 copy-done.1
  69.2 0.2 shard_map.52
  69.4 18.7 %all_to_all.36 = f32[16,48,128]{2,1,0:T(8,128)S(1)} all-to-all(f32[16,48,128]{2,1,0:T(8,128)S(1)} %get-tuple-element.17), channel_id=1, replica_groups=mesh['z_far'=4,'z_near'=2,'y_far'=4,'y_near'=2,'x'=4,'core'=2] {'z_far',..., dimensions={0} | all-to-all | bytes 786432 | tf_op jit(solution)/shard_map/all_to_all | solution.py:265
  88.1 6.2 %all-gather.1.got_ref = f32[32,48,128]{2,1,0:T(8,128)S(1)} all-gather(f32[16,48,128]{2,1,0:T(8,128)S(1)} %all_to_all.36), channel_id=3, replica_groups=mesh['z_far'=4,'z_near'=2,'y_far'=4,'y_near'=2,'x'=4,'core'=2] {'core'}, dimensions={0}, use_global_device_ids=true | all-gather | bytes 1179648 | tf_op jit(solution)/shard_map/all_gather | solution.py:268
  94.3 2.9 %shard_map.53 = f32[16,56,128]{2,1,0:T(8,128)S(1)} custom-call(f32[32,48,128]{2,1,0:T(8,128)S(1)} %all-gather.1.got_ref, f32[32,56,128]{2,1,0:T(8,128)S(1)} %all-gather.col_ref, bf16[1024,2048]{1,0:T(8,128)(2,1)S(1)} %get-tuple-element.18.high_ref, bf16[1024,2048]{1,0:T(8,128)(2,1)S(1)} %get-tuple-element.19.low_ref), custom_call_target="tpu_custom_call" | custom-call | tf_op jit(solution)/shard_map/pallas_call | solution.py:293
  97.2 12.5 %all_to_all.37.got_ref = f32[16,56,128]{2,1,0:T(8,128)S(1)} all-to-all(f32[16,56,128]{2,1,0:T(8,128)S(1)} %shard_map.53), channel_id=1, replica_groups=mesh['z_far'=4,'z_near'=2,'y_far'=4,'y_near'=2,'x'=4,'core'=2] {'z_near'..., dimensions={0} | all-to-all | bytes 917504 | tf_op jit(solution)/shard_map/all_to_all | solution.py:265
  109.7 0.1 shard_map.54
  109.9 11.4 %all_to_all.38.got_ref = f32[32,8,128]{2,1,0:T(8,128)S(1)} all-to-all(f32[32,8,128]{2,1,0:T(8,128)S(1)} %get-tuple-element.21), channel_id=1, replica_groups=mesh['z_far'=4,'z_near'=2,'y_far'=4,'y_near'=2,'x'=4,'core'=2] {'z_near'..., dimensions={0} | all-to-all | bytes 262144 | tf_op jit(solution)/shard_map/all_to_all | solution.py:265
  121.4 16.0 %all_to_all.39.got_ref = f32[16,8,128]{2,1,0:T(8,128)S(1)} all-to-all(f32[16,8,128]{2,1,0:T(8,128)S(1)} %shard_map.55), channel_id=1, replica_groups=mesh['z_far'=4,'z_near'=2,'y_far'=4,'y_near'=2,'x'=4,'core'=2] {'z_far',..., dimensions={0} | all-to-all | bytes 131072 | tf_op jit(solution)/shard_map/all_to_all | solution.py:265
  137.3 0.7 shard_map.56
  (1 shorter events, 0.0 us)
Async XLA Ops:
  0.6 0.8 copy-start
  1.4 0.7 copy-start.2
  2.1 67.1 %copy-start.1 = (f32[96,64]{0,1:T(8,128)S(1)}, f32[96,64]{0,1:T(8,128)}, u32[]{:S(2)}) copy-start(f32[96,64]{0,1:T(8,128)} %param.3) | copy-start | bytes 73732
  3.0 33.3 %all-to-all-start = ((f32[16,56,128]{2,1,0:T(8,128)}), f32[16,56,128]{2,1,0:T(8,128)S(1)}, u32[]{:S(2)}, u32[]{:S(2)}) async-start(f32[16,56,128]{2,1,0:T(8,128)} %get-tuple-element.14), calls=%async_computation | async-start | bytes 917504 | tf_op jit(solution)/shard_map/all_to_all | solution.py:265
  36.3 11.2 %all-to-all-start.1 = ((f32[16,8,128]{2,1,0:T(8,128)}), f32[16,8,128]{2,1,0:T(8,128)S(1)}, u32[]{:S(2)}, u32[]{:S(2)}) async-start(f32[16,8,128]{2,1,0:T(8,128)} %get-tuple-element.15), calls=%async_computation.1 | async-start | bytes 131072 | tf_op jit(solution)/shard_map/all_to_all | solution.py:265

commit v5 on v4

--- a/solution.py
+++ b/solution.py
@@ -20,7 +20,8 @@
 F32 = jnp.float32
 AXES = {"z_far": 4, "z_near": 2, "y_far": 4, "y_near": 2, "x": 4, "core": 2}
 FAR, FAR_SIZE = ("z_far", "y_far"), 16
-MID, MID_SIZE = ("z_near", "y_near", "x"), 16
+PAIRS, PAIRS_SIZE = ("z_near", "y_near"), 4
+MID, MID_SIZE = PAIRS + ("x",), 16
 NEAR, NEAR_SIZE = MID + ("core",), 32
 GATHERED = 2 * FAR_SIZE
 ROWS, COLS = MID_SIZE * MICS, GATHERED * MICS
@@ -83,7 +84,7 @@
     points = widen(points)
     block = jnp.concatenate([pack(field_ref[...]), points], axis=0)
     col_ref[...] = jnp.broadcast_to(block[None], col_ref.shape)
-    row_ref[...] = jnp.broadcast_to(points[None], row_ref.shape)
+    row_ref[...] = points
 
 
 def factors(points, wave, of_rows):
@@ -107,9 +108,8 @@
     return jnp.concatenate(rows + rest + [blank], axis=0)
 
 
-def points_of(ref, count, first):
-    tiles = [ref[i, first : first + EXTRA, :MICS] for i in range(count)]
-    return jnp.concatenate(tiles, axis=1)
+def side_by_side(tiles):
+    return jnp.concatenate([tile[:, :MICS] for tile in tiles], axis=1)
 
 
 def sinc_of(turns2):
@@ -142,7 +142,20 @@
 
 
 def first_kernel(
-    col_ref, row_ref, wave_ref, out_ref, high_ref, low_ref, weights_ref, col_f, row_f
+    col_ref,
+    row_ref,
+    row1_ref,
+    row2_ref,
+    row3_ref,
+    place_ref,
+    wave_ref,
+    out_ref,
+    high_ref,
+    low_ref,
+    weights_ref,
+    col_f,
+    row_f,
+    tiles_ref,
 ):
     wave = wave_ref[0]
 
@@ -151,8 +164,12 @@
         return carry
 
     lax.fori_loop(0, GATHERED, place, 0, unroll=True)
-    col_f[...] = factors(points_of(col_ref, GATHERED, PACKED), wave, False).astype(BF16)
-    row_f[...] = factors(points_of(row_ref, MID_SIZE, 0), wave, True).T.astype(BF16)
+    cols = side_by_side([col_ref[i, PACKED:, :] for i in range(GATHERED)])
+    col_f[...] = factors(cols, wave, False).astype(BF16)
+    for i, ref in enumerate((row_ref, row1_ref, row2_ref, row3_ref)):
+        tiles_ref[i * PAIRS_SIZE : (i + 1) * PAIRS_SIZE] = ref[...]
+    rows = side_by_side([tiles_ref[place_ref[i]] for i in range(MID_SIZE)])
+    row_f[...] = factors(rows, wave, True).T.astype(BF16)
 
     def some_rows(index, carry):
         at = pl.ds(pl.multiple_of(index * STEP, STEP), STEP)
@@ -232,7 +249,7 @@
     keep_ref[2] = direction
     keep_ref[3] = turned
     norm_ref[...] = rows_of(norm_next)
-    along = rows_of(over_rows(direction * turned))
+    along = over_rows(direction * turned)
     send_ref[...] = jnp.broadcast_to(along[None], send_ref.shape)
 
 
@@ -242,7 +259,7 @@
 
 
 def end_kernel(got_ref, norm_ref, keep_ref, solution_ref, residual_ref):
-    along = jnp.sum(got_ref[:, 0:1, :], axis=0)
+    along = jnp.sum(got_ref[...], axis=0)
     alpha = norm_ref[0:1] / along
     solution_ref[...] = (keep_ref[0] + alpha * keep_ref[2])[:, :FRAMES]
     residual_ref[...] = (keep_ref[1] - alpha * keep_ref[3])[:, :FRAMES]
@@ -257,6 +274,24 @@
     )
 
 
+def points_of_mid(points):
+    pair = 2 * lax.axis_index("z_near") + lax.axis_index("y_near")
+    column = lax.axis_index("x")
+    columns = AXES["x"]
+
+    def across(value, bits):
+        return lax.ppermute(value, PAIRS, [(i, i ^ bits) for i in range(PAIRS_SIZE)])
+
+    def along(value, step):
+        return lax.ppermute(value, "x", [(i, (i + step) % columns) for i in range(columns)])
+
+    four = jnp.stack([points] + [across(points, bits) for bits in range(1, PAIRS_SIZE)])
+    every = [four] + [along(four, step) for step in range(1, columns)]
+    index = lax.iota(jnp.int32, MID_SIZE)
+    back = (column - index % columns) % columns
+    return *every, back * PAIRS_SIZE + ((index // columns) ^ pair)
+
+
 def local(right_side, positions, wavenumber):
     field = right_side.T
     block = (MICS, LANES)
@@ -272,21 +307,22 @@
     vector = pl.BlockSpec(memory_space=pltpu.VMEM)
     to_cols, points = call(
         start_kernel,
-        [((FAR_SIZE, PACKED + EXTRA, LANES), F32), ((MID_SIZE, EXTRA, LANES), F32)],
+        [((FAR_SIZE, PACKED + EXTRA, LANES), F32), ((EXTRA, LANES), F32)],
     )(field, positions)
     col_blocks = gather(to_cols)
-    row_points = exchange(points, MID)
+    row_points = points_of_mid(points)
 
     partial, high, low = call(
         first_kernel,
         [((MID_SIZE, PACKED, LANES), F32), ((ROWS, COLS), BF16), ((ROWS, COLS), BF16)],
-        in_specs=[vector, vector, scalar],
+        in_specs=[vector] * 5 + [scalar] * 2,
         scratch_shapes=[
             pltpu.VMEM((COLS, 2 * LANES), BF16),
             pltpu.VMEM((DEPTH, COLS), BF16),
             pltpu.VMEM((ROWS, DEPTH), BF16),
+            pltpu.VMEM((MID_SIZE, EXTRA, LANES), F32),
         ],
-    )(col_blocks, row_points, wavenumber)
+    )(col_blocks, *row_points, wavenumber)
     image, to_cols = call(image_kernel, [(block, F32), ((FAR_SIZE, PACKED, LANES), F32)])(
         exchange(partial, MID), field
     )
@@ -301,9 +337,9 @@
     )(gather(to_cols), col_blocks, high, low)
     keep, norm_next, send = call(
         direction_kernel,
-        [((4,) + block, F32), ((EXTRA, LANES), F32), ((NEAR_SIZE, EXTRA, LANES), F32)],
+        [((4,) + block, F32), ((EXTRA, LANES), F32), ((NEAR_SIZE, 1, LANES), F32)],
     )(exchange(partial, MID), field, image)
-    (send,) = call(relay_kernel, [((FAR_SIZE, EXTRA, LANES), F32)])(exchange(send, NEAR))
+    (send,) = call(relay_kernel, [((FAR_SIZE, 1, LANES), F32)])(exchange(send, NEAR))
     solution_field, residual = call(
         end_kernel, [((MICS, FRAMES), F32), ((MICS, FRAMES), F32)]
     )(exchange(send, FAR), norm_next, keep)

time: 139 us -> 142 us (1.022)
  waiting for transfers between devices: 18 us -> 0.98 us
  starting transfers between devices: 21.2 us -> 33.9 us
  blocking collectives: 82.1 us -> 88.6 us
    all_to_all x2 -> x1, waiting for transfers between devices: 18 us -> 0.01 us  [exchange(): return lax.all_to_all(value, axis, 0, 0)]
    ppermute x0 -> x6, starting transfers between devices: none -> 17.7 us  [the longest x3 9.32 us: along(): lax.ppermute(value, 'x', [(i, (i + step) % columns) for i in range(column...]
    all_to_all x5, blocking collectives: 71.3 us -> 77.9 us  [exchange(): return lax.all_to_all(value, axis, 0, 0)]
    all_to_all x2 -> x1, starting transfers between devices: 21.2 us -> 16.2 us  [exchange(): return lax.all_to_all(value, axis, 0, 0)]
  transfers between devices with their start and end apart: 2 -> 7, of which waited for: 2 -> 1; matrix products, arithmetic and copies ran while one was open for 0% -> 0% of each run, Pallas kernels for 0% -> 0%
where the time goes in v5:
time: 142 us; the launch traced here: 141 us
  blocking collectives  88.6 us (62%)
  starting transfers between devices  33.9 us (24%)
  Pallas kernels  14.5 us (10%)
  local copies, waits for them, and re-layouts  1.44 us (1%)
    all_to_all x5, blocking collectives, exchange(): return lax.all_to_all(value, axis, 0, 0)  77.9 us
    all_to_all x1, starting transfers between devices, exchange(): return lax.all_to_all(value, axis, 0, 0)  16.2 us
    all_gather x2, blocking collectives, gather(): both = lax.all_gather(exchange(value, FAR), 'core')  10.8 us
    pallas_call x1, Pallas kernels, local(): call(first_kernel, [((MID_SIZE, PACKED, LANES), F32), ((ROWS, COLS), BF16...  9.54 us
    ppermute x3, starting transfers between devices, along(): lax.ppermute(value, 'x', [(i, (i + step) % columns) for i in range(column...  9.32 us
    ppermute x3, starting transfers between devices, across(): lax.ppermute(value, PAIRS, [(i, i ^ bits) for i in range(PAIRS_SIZE)])  8.37 us
    pallas_call x1, Pallas kernels, local(): call(second_kernel, [((MID_SIZE, PACKED + EXTRA, LANES), F32)], scratch_s...  3 us
  transfers between devices with their start and end apart: 7, of which 1 were waited for; matrix products, arithmetic and copies ran while one was open for 0% of the time, Pallas kernels for 0%

profile of v5, /device:TPU:1, one launch (start us, length us, event | category | flops | bytes accessed | tf_op | source)
XLA Modules:
  0.0 140.9 jit_solution(17462576727818683619)
XLA Ops:
  0.6 0.0 copy-start
  0.6 0.7 copy-done
  1.4 0.0 copy-start.2
  1.4 0.7 copy-done.2
  2.1 0.0 copy-start.1
  2.1 0.9 shard_map.50
  3.0 16.2 %all-to-all-start = ((f32[16,56,128]{2,1,0:T(8,128)}), f32[16,56,128]{2,1,0:T(8,128)S(1)}, u32[]{:S(2)}, u32[]{:S(2)}) async-start(f32[16,56,128]{2,1,0:T(8,128)} %get-tuple-element.14), calls=%async_computation | async-start | bytes 917504 | tf_op jit(solution)/shard_map/all_to_all | solution.py:300
  19.2 3.2 %collective-permute-start.2 = (f32[8,128]{1,0:T(8,128)S(1)}, f32[8,128]{1,0:T(8,128)S(1)}, u32[]{:S(2)}, u32[]{:S(2)}) collective-permute-start(f32[8,128]{1,0:T(8,128)S(1)} %get-tuple-element.15), channel_id=1, source_target_pairs={{0,72},{8,64},{64,8},{72,0},{1,73},{9,65},{65,9},{73,1},{2,74},{10... | collective-permute-start | bytes 12296 | tf_op jit(solution)/shard_map/ppermute | solution.py:283
  22.4 2.2 %collective-permute-start.1 = (f32[8,128]{1,0:T(8,128)S(1)}, f32[8,128]{1,0:T(8,128)S(1)}, u32[]{:S(2)}, u32[]{:S(2)}) collective-permute-start(f32[8,128]{1,0:T(8,128)S(1)} %get-tuple-element.15), channel_id=1, source_target_pairs={{0,64},{8,72},{64,0},{72,8},{1,65},{9,73},{65,1},{73,9},{2,66},{10... | collective-permute-start | bytes 12296 | tf_op jit(solution)/shard_map/ppermute | solution.py:283
  24.6 3.0 %collective-permute-start = (f32[8,128]{1,0:T(8,128)S(1)}, f32[8,128]{1,0:T(8,128)S(1)}, u32[]{:S(2)}, u32[]{:S(2)}) collective-permute-start(f32[8,128]{1,0:T(8,128)S(1)} %get-tuple-element.15), channel_id=1, source_target_pairs={{0,8},{8,0},{64,72},{72,64},{1,9},{9,1},{65,73},{73,65},{2,10},{10... | collective-permute-start | bytes 12296 | tf_op jit(solution)/shard_map/ppermute | solution.py:283
  28.3 0.0 collective-permute-done.2
  28.3 0.0 collective-permute-done.1
  28.3 1.0 collective-permute-done
  29.3 4.4 %collective-permute-start.5 = (f32[4,8,128]{2,1,0:T(8,128)S(1)}, f32[4,8,128]{2,1,0:T(8,128)S(1)}, u32[]{:S(2)}, u32[]{:S(2)}) collective-permute-start(f32[4,8,128]{2,1,0:T(8,128)S(1)} %pad_maximum_fusion.row_ref), channel_id=1, source_target_pairs={{0,6},{2,0},{4,2},{6,4},{1,7},{3,1},{5,3},{7,5},{8,14},{10,8},{12,... | collective-permute-start | bytes 49160 | tf_op jit(solution)/shard_map/ppermute | solution.py:286
  33.7 2.4 %collective-permute-start.4 = (f32[4,8,128]{2,1,0:T(8,128)S(1)}, f32[4,8,128]{2,1,0:T(8,128)S(1)}, u32[]{:S(2)}, u32[]{:S(2)}) collective-permute-start(f32[4,8,128]{2,1,0:T(8,128)S(1)} %pad_maximum_fusion.row_ref), channel_id=1, source_target_pairs={{0,4},{2,6},{4,0},{6,2},{1,5},{3,7},{5,1},{7,3},{8,12},{10,14},{12... | collective-permute-start | bytes 49160 | tf_op jit(solution)/shard_map/ppermute | solution.py:286
  36.1 2.5 %collective-permute-start.3 = (f32[4,8,128]{2,1,0:T(8,128)S(1)}, f32[4,8,128]{2,1,0:T(8,128)S(1)}, u32[]{:S(2)}, u32[]{:S(2)}) collective-permute-start(f32[4,8,128]{2,1,0:T(8,128)S(1)} %pad_maximum_fusion.row_ref), channel_id=1, source_target_pairs={{0,2},{2,4},{4,6},{6,0},{1,3},{3,5},{5,7},{7,1},{8,10},{10,12},{12... | collective-permute-start | bytes 49160 | tf_op jit(solution)/shard_map/ppermute | solution.py:286
  38.6 0.0 all-to-all-done
  38.6 5.7 %all-gather.col_ref = f32[32,56,128]{2,1,0:T(8,128)S(1)} all-gather(f32[16,56,128]{2,1,0:T(8,128)S(1)} %all-to-all-done), channel_id=2, replica_groups=mesh['z_far'=4,'z_near'=2,'y_far'=4,'y_near'=2,'x'=4,'core'=2] {'core'}, dimensions={0}, use_global_device_ids=true | all-gather | bytes 1376256 | tf_op jit(solution)/shard_map/all_gather | solution.py:303
  44.3 0.0 collective-permute-done.5.row3_ref
  44.3 0.0 collective-permute-done.4.row2_ref
  44.3 0.0 collective-permute-done.3.row1_ref
  44.3 9.5 %shard_map.51 = (f32[16,48,128]{2,1,0:T(8,128)S(1)}, bf16[1024,2048]{1,0:T(8,128)(2,1)S(1)}, bf16[1024,2048]{1,0:T(8,128)(2,1)S(1)}) custom-call(f32[32,56,128]{2,1,0:T(8,128)S(1)} %all-gather.col_ref, f32[4,8,128]{2,1,0:T(8,128)S(1)} %pad_maximum_fusion.row_ref, f32[4,8,128]{2,1,0:T(8,128)S(1)} %collective-permute-done.3.row1_ref, ...), custom_call_target="tpu_custom_call" | custom-call | tf_op jit(solution)/shard_map/pallas_call | solution.py:315
  53.9 13.0 %all_to_all.30.got_ref = f32[16,48,128]{2,1,0:T(8,128)S(1)} all-to-all(f32[16,48,128]{2,1,0:T(8,128)S(1)} %get-tuple-element.16), channel_id=1, replica_groups=mesh['z_far'=4,'z_near'=2,'y_far'=4,'y_near'=2,'x'=4,'core'=2] {'z_near'..., dimensions={0} | all-to-all | bytes 786432 | tf_op jit(solution)/shard_map/all_to_all | solution.py:300
  66.9 0.0 copy-done.1
  66.9 0.2 shard_map.52
  67.1 26.3 %all_to_all.31 = f32[16,48,128]{2,1,0:T(8,128)S(1)} all-to-all(f32[16,48,128]{2,1,0:T(8,128)S(1)} %get-tuple-element.17), channel_id=1, replica_groups=mesh['z_far'=4,'z_near'=2,'y_far'=4,'y_near'=2,'x'=4,'core'=2] {'z_far',..., dimensions={0} | all-to-all | bytes 786432 | tf_op jit(solution)/shard_map/all_to_all | solution.py:300
  93.4 5.1 %all-gather.1.got_ref = f32[32,48,128]{2,1,0:T(8,128)S(1)} all-gather(f32[16,48,128]{2,1,0:T(8,128)S(1)} %all_to_all.31), channel_id=3, replica_groups=mesh['z_far'=4,'z_near'=2,'y_far'=4,'y_near'=2,'x'=4,'core'=2] {'core'}, dimensions={0}, use_global_device_ids=true | all-gather | bytes 1179648 | tf_op jit(solution)/shard_map/all_gather | solution.py:303
  98.5 3.0 %shard_map.53 = f32[16,56,128]{2,1,0:T(8,128)S(1)} custom-call(f32[32,48,128]{2,1,0:T(8,128)S(1)} %all-gather.1.got_ref, f32[32,56,128]{2,1,0:T(8,128)S(1)} %all-gather.col_ref, bf16[1024,2048]{1,0:T(8,128)(2,1)S(1)} %get-tuple-element.18.high_ref, bf16[1024,2048]{1,0:T(8,128)(2,1)S(1)} %get-tuple-element.19.low_ref), custom_call_target="tpu_custom_call" | custom-call | tf_op jit(solution)/shard_map/pallas_call | solution.py:329
  101.5 12.4 %all_to_all.32.got_ref = f32[16,56,128]{2,1,0:T(8,128)S(1)} all-to-all(f32[16,56,128]{2,1,0:T(8,128)S(1)} %shard_map.53), channel_id=1, replica_groups=mesh['z_far'=4,'z_near'=2,'y_far'=4,'y_near'=2,'x'=4,'core'=2] {'z_near'..., dimensions={0} | all-to-all | bytes 917504 | tf_op jit(solution)/shard_map/all_to_all | solution.py:300
  113.9 0.1 shard_map.54
  114.1 10.7 %all_to_all.33.got_ref = f32[32,1,128]{2,1,0:T(1,128)S(1)} all-to-all(f32[32,1,128]{2,1,0:T(1,128)S(1)} %get-tuple-element.21), channel_id=1, replica_groups=mesh['z_far'=4,'z_near'=2,'y_far'=4,'y_near'=2,'x'=4,'core'=2] {'z_near'..., dimensions={0} | all-to-all | bytes 32768 | tf_op jit(solution)/shard_map/all_to_all | solution.py:300
  124.9 15.4 %all_to_all.34.got_ref = f32[16,1,128]{2,1,0:T(1,128)S(1)} all-to-all(f32[16,1,128]{2,1,0:T(1,128)S(1)} %shard_map.55), channel_id=1, replica_groups=mesh['z_far'=4,'z_near'=2,'y_far'=4,'y_near'=2,'x'=4,'core'=2] {'z_far',..., dimensions={0} | all-to-all | bytes 16384 | tf_op jit(solution)/shard_map/all_to_all | solution.py:300
  140.3 0.7 shard_map.56
  (3 shorter events, 0.1 us)
Async XLA Ops:
  0.6 0.8 copy-start
  1.4 0.7 copy-start.2
  2.1 64.8 %copy-start.1 = (f32[96,64]{0,1:T(8,128)S(1)}, f32[96,64]{0,1:T(8,128)}, u32[]{:S(2)}) copy-start(f32[96,64]{0,1:T(8,128)} %param.3) | copy-start | bytes 73732
  3.0 35.6 %all-to-all-start = ((f32[16,56,128]{2,1,0:T(8,128)}), f32[16,56,128]{2,1,0:T(8,128)S(1)}, u32[]{:S(2)}, u32[]{:S(2)}) async-start(f32[16,56,128]{2,1,0:T(8,128)} %get-tuple-element.14), calls=%async_computation | async-start | bytes 917504 | tf_op jit(solution)/shard_map/all_to_all | solution.py:300
  19.2 9.1 %collective-permute-start.2 = (f32[8,128]{1,0:T(8,128)S(1)}, f32[8,128]{1,0:T(8,128)S(1)}, u32[]{:S(2)}, u32[]{:S(2)}) collective-permute-start(f32[8,128]{1,0:T(8,128)S(1)} %get-tuple-element.15), channel_id=1, source_target_pairs={{0,72},{8,64},{64,8},{72,0},{1,73},{9,65},{65,9},{73,1},{2,74},{10... | collective-permute-start | bytes 12296 | tf_op jit(solution)/shard_map/ppermute | solution.py:283
  22.4 5.9 %collective-permute-start.1 = (f32[8,128]{1,0:T(8,128)S(1)}, f32[8,128]{1,0:T(8,128)S(1)}, u32[]{:S(2)}, u32[]{:S(2)}) collective-permute-start(f32[8,128]{1,0:T(8,128)S(1)} %get-tuple-element.15), channel_id=1, source_target_pairs={{0,64},{8,72},{64,0},{72,8},{1,65},{9,73},{65,1},{73,9},{2,66},{10... | collective-permute-start | bytes 12296 | tf_op jit(solution)/shard_map/ppermute | solution.py:283
  24.6 4.6 %collective-permute-start = (f32[8,128]{1,0:T(8,128)S(1)}, f32[8,128]{1,0:T(8,128)S(1)}, u32[]{:S(2)}, u32[]{:S(2)}) collective-permute-start(f32[8,128]{1,0:T(8,128)S(1)} %get-tuple-element.15), channel_id=1, source_target_pairs={{0,8},{8,0},{64,72},{72,64},{1,9},{9,1},{65,73},{73,65},{2,10},{10... | collective-permute-start | bytes 12296 | tf_op jit(solution)/shard_map/ppermute | solution.py:283
  29.3 15.1 %collective-permute-start.5 = (f32[4,8,128]{2,1,0:T(8,128)S(1)}, f32[4,8,128]{2,1,0:T(8,128)S(1)}, u32[]{:S(2)}, u32[]{:S(2)}) collective-permute-start(f32[4,8,128]{2,1,0:T(8,128)S(1)} %pad_maximum_fusion.row_ref), channel_id=1, source_target_pairs={{0,6},{2,0},{4,2},{6,4},{1,7},{3,1},{5,3},{7,5},{8,14},{10,8},{12,... | collective-permute-start | bytes 49160 | tf_op jit(solution)/shard_map/ppermute | solution.py:286
  33.7 10.7 %collective-permute-start.4 = (f32[4,8,128]{2,1,0:T(8,128)S(1)}, f32[4,8,128]{2,1,0:T(8,128)S(1)}, u32[]{:S(2)}, u32[]{:S(2)}) collective-permute-start(f32[4,8,128]{2,1,0:T(8,128)S(1)} %pad_maximum_fusion.row_ref), channel_id=1, source_target_pairs={{0,4},{2,6},{4,0},{6,2},{1,5},{3,7},{5,1},{7,3},{8,12},{10,14},{12... | collective-permute-start | bytes 49160 | tf_op jit(solution)/shard_map/ppermute | solution.py:286
  36.1 8.2 %collective-permute-start.3 = (f32[4,8,128]{2,1,0:T(8,128)S(1)}, f32[4,8,128]{2,1,0:T(8,128)S(1)}, u32[]{:S(2)}, u32[]{:S(2)}) collective-permute-start(f32[4,8,128]{2,1,0:T(8,128)S(1)} %pad_maximum_fusion.row_ref), channel_id=1, source_target_pairs={{0,2},{2,4},{4,6},{6,0},{1,3},{3,5},{5,7},{7,1},{8,10},{10,12},{12... | collective-permute-start | bytes 49160 | tf_op jit(solution)/shard_map/ppermute | solution.py:286

commit v6 on v4

--- a/solution.py
+++ b/solution.py
@@ -21,7 +21,8 @@
 AXES = {"z_far": 4, "z_near": 2, "y_far": 4, "y_near": 2, "x": 4, "core": 2}
 FAR, FAR_SIZE = ("z_far", "y_far"), 16
 MID, MID_SIZE = ("z_near", "y_near", "x"), 16
-NEAR, NEAR_SIZE = MID + ("core",), 32
+FIRST, FIRST_SIZE = ("z_far", "z_near", "core"), 16
+LAST, LAST_SIZE = ("y_far", "y_near", "x"), 32
 GATHERED = 2 * FAR_SIZE
 ROWS, COLS = MID_SIZE * MICS, GATHERED * MICS
 SINC = (
@@ -232,7 +233,7 @@
     keep_ref[2] = direction
     keep_ref[3] = turned
     norm_ref[...] = rows_of(norm_next)
-    along = rows_of(over_rows(direction * turned))
+    along = over_rows(direction * turned)
     send_ref[...] = jnp.broadcast_to(along[None], send_ref.shape)
 
 
@@ -242,7 +243,7 @@
 
 
 def end_kernel(got_ref, norm_ref, keep_ref, solution_ref, residual_ref):
-    along = jnp.sum(got_ref[:, 0:1, :], axis=0)
+    along = jnp.sum(got_ref[...], axis=0)
     alpha = norm_ref[0:1] / along
     solution_ref[...] = (keep_ref[0] + alpha * keep_ref[2])[:, :FRAMES]
     residual_ref[...] = (keep_ref[1] - alpha * keep_ref[3])[:, :FRAMES]
@@ -301,12 +302,12 @@
     )(gather(to_cols), col_blocks, high, low)
     keep, norm_next, send = call(
         direction_kernel,
-        [((4,) + block, F32), ((EXTRA, LANES), F32), ((NEAR_SIZE, EXTRA, LANES), F32)],
+        [((4,) + block, F32), ((EXTRA, LANES), F32), ((FIRST_SIZE, 1, LANES), F32)],
     )(exchange(partial, MID), field, image)
-    (send,) = call(relay_kernel, [((FAR_SIZE, EXTRA, LANES), F32)])(exchange(send, NEAR))
+    (send,) = call(relay_kernel, [((LAST_SIZE, 1, LANES), F32)])(exchange(send, FIRST))
     solution_field, residual = call(
         end_kernel, [((MICS, FRAMES), F32), ((MICS, FRAMES), F32)]
-    )(exchange(send, FAR), norm_next, keep)
+    )(exchange(send, LAST), norm_next, keep)
     return solution_field.T, residual.T
 
 

time: 139 us -> 135 us (0.971)
  blocking collectives: 82.1 us -> 78.6 us
    all_to_all x5, blocking collectives: 71.3 us -> 67.7 us  [exchange(): return lax.all_to_all(value, axis, 0, 0)]
where the time goes in v6:
time: 135 us; the launch traced here: 134 us
  blocking collectives  78.6 us (58%)
  starting transfers between devices  21.2 us (16%)
  waiting for transfers between devices  18 us (13%)
  Pallas kernels  13.9 us (10%)
  local copies, waits for them, and re-layouts  1.44 us (1%)
    all_to_all x5, blocking collectives, exchange(): return lax.all_to_all(value, axis, 0, 0)  67.7 us
    all_to_all x2, starting transfers between devices, exchange(): return lax.all_to_all(value, axis, 0, 0)  21.2 us
    all_to_all x2, waiting for transfers between devices, exchange(): return lax.all_to_all(value, axis, 0, 0)  18 us
    all_gather x2, blocking collectives, gather(): both = lax.all_gather(exchange(value, FAR), 'core')  10.8 us
    pallas_call x1, Pallas kernels, local(): call(first_kernel, [((MID_SIZE, PACKED, LANES), F32), ((ROWS, COLS), BF16...  8.94 us
    pallas_call x1, Pallas kernels, local(): call(second_kernel, [((MID_SIZE, PACKED + EXTRA, LANES), F32)], scratch_s...  2.92 us
  transfers between devices with their start and end apart: 2, of which 2 were waited for; matrix products, arithmetic and copies ran while one was open for 0% of the time, Pallas kernels for 0%

profile of v6, /device:TPU:1, one launch (start us, length us, event | category | flops | bytes accessed | tf_op | source)
XLA Modules:
  0.0 134.4 jit_solution(5097888898123173426)
XLA Ops:
  0.6 0.0 copy-start
  0.6 0.7 copy-done
  1.4 0.0 copy-start.2
  1.4 0.7 copy-done.2
  2.1 0.0 copy-start.1
  2.1 0.9 shard_map.50
  3.0 16.2 %all-to-all-start = ((f32[16,56,128]{2,1,0:T(8,128)}), f32[16,56,128]{2,1,0:T(8,128)S(1)}, u32[]{:S(2)}, u32[]{:S(2)}) async-start(f32[16,56,128]{2,1,0:T(8,128)} %get-tuple-element.14), calls=%async_computation | async-start | bytes 917504 | tf_op jit(solution)/shard_map/all_to_all | solution.py:266
  19.9 16.4 %all-to-all-done = f32[16,56,128]{2,1,0:T(8,128)S(1)} async-done(((f32[16,56,128]{2,1,0:T(8,128)}), f32[16,56,128]{2,1,0:T(8,128)S(1)}, u32[]{:S(2)}, u32[]{:S(2)}) %all-to-all-start) | async-done | bytes 458784 | tf_op jit(solution)/shard_map/all_to_all | solution.py:266
  36.3 5.0 %all-to-all-start.1 = ((f32[16,8,128]{2,1,0:T(8,128)}), f32[16,8,128]{2,1,0:T(8,128)S(1)}, u32[]{:S(2)}, u32[]{:S(2)}) async-start(f32[16,8,128]{2,1,0:T(8,128)} %get-tuple-element.15), calls=%async_computation.1 | async-start | bytes 131072 | tf_op jit(solution)/shard_map/all_to_all | solution.py:266
  41.4 4.7 %all-gather.col_ref = f32[32,56,128]{2,1,0:T(8,128)S(1)} all-gather(f32[16,56,128]{2,1,0:T(8,128)S(1)} %all-to-all-done), channel_id=2, replica_groups=mesh['z_far'=4,'z_near'=2,'y_far'=4,'y_near'=2,'x'=4,'core'=2] {'core'}, dimensions={0}, use_global_device_ids=true | all-gather | bytes 1376256 | tf_op jit(solution)/shard_map/all_gather | solution.py:269
  46.0 1.5 %all-to-all-done.1.row_ref = f32[16,8,128]{2,1,0:T(8,128)S(1)} async-done(((f32[16,8,128]{2,1,0:T(8,128)}), f32[16,8,128]{2,1,0:T(8,128)S(1)}, u32[]{:S(2)}, u32[]{:S(2)}) %all-to-all-start.1) | async-done | bytes 65568 | tf_op jit(solution)/shard_map/all_to_all | solution.py:266
  47.5 8.9 %shard_map.51 = (f32[16,48,128]{2,1,0:T(8,128)S(1)}, bf16[1024,2048]{1,0:T(8,128)(2,1)S(1)}, bf16[1024,2048]{1,0:T(8,128)(2,1)S(1)}) custom-call(f32[32,56,128]{2,1,0:T(8,128)S(1)} %all-gather.col_ref, f32[16,8,128]{2,1,0:T(8,128)S(1)} %all-to-all-done.1.row_ref, f32[1]{0:T(128)S(6)} %copy.5.wave_ref), custom_call_target="tpu_custom_call" | custom-call | tf_op jit(solution)/shard_map/pallas_call | solution.py:281
  56.5 12.7 %all_to_all.35.got_ref = f32[16,48,128]{2,1,0:T(8,128)S(1)} all-to-all(f32[16,48,128]{2,1,0:T(8,128)S(1)} %get-tuple-element.16), channel_id=1, replica_groups=mesh['z_far'=4,'z_near'=2,'y_far'=4,'y_near'=2,'x'=4,'core'=2] {'z_near'..., dimensions={0} | all-to-all | bytes 786432 | tf_op jit(solution)/shard_map/all_to_all | solution.py:266
  69.2 0.0 copy-done.1
  69.2 0.2 shard_map.52
  69.4 18.7 %all_to_all.36 = f32[16,48,128]{2,1,0:T(8,128)S(1)} all-to-all(f32[16,48,128]{2,1,0:T(8,128)S(1)} %get-tuple-element.17), channel_id=1, replica_groups=mesh['z_far'=4,'z_near'=2,'y_far'=4,'y_near'=2,'x'=4,'core'=2] {'z_far',..., dimensions={0} | all-to-all | bytes 786432 | tf_op jit(solution)/shard_map/all_to_all | solution.py:266
  88.1 6.2 %all-gather.1.got_ref = f32[32,48,128]{2,1,0:T(8,128)S(1)} all-gather(f32[16,48,128]{2,1,0:T(8,128)S(1)} %all_to_all.36), channel_id=3, replica_groups=mesh['z_far'=4,'z_near'=2,'y_far'=4,'y_near'=2,'x'=4,'core'=2] {'core'}, dimensions={0}, use_global_device_ids=true | all-gather | bytes 1179648 | tf_op jit(solution)/shard_map/all_gather | solution.py:269
  94.3 2.9 %shard_map.53 = f32[16,56,128]{2,1,0:T(8,128)S(1)} custom-call(f32[32,48,128]{2,1,0:T(8,128)S(1)} %all-gather.1.got_ref, f32[32,56,128]{2,1,0:T(8,128)S(1)} %all-gather.col_ref, bf16[1024,2048]{1,0:T(8,128)(2,1)S(1)} %get-tuple-element.18.high_ref, bf16[1024,2048]{1,0:T(8,128)(2,1)S(1)} %get-tuple-element.19.low_ref), custom_call_target="tpu_custom_call" | custom-call | tf_op jit(solution)/shard_map/pallas_call | solution.py:294
  97.2 12.5 %all_to_all.37.got_ref = f32[16,56,128]{2,1,0:T(8,128)S(1)} all-to-all(f32[16,56,128]{2,1,0:T(8,128)S(1)} %shard_map.53), channel_id=1, replica_groups=mesh['z_far'=4,'z_near'=2,'y_far'=4,'y_near'=2,'x'=4,'core'=2] {'z_near'..., dimensions={0} | all-to-all | bytes 917504 | tf_op jit(solution)/shard_map/all_to_all | solution.py:266
  109.7 0.1 shard_map.54
  109.9 12.0 %all_to_all.38.got_ref = f32[16,1,128]{2,1,0:T(1,128)S(1)} all-to-all(f32[16,1,128]{2,1,0:T(1,128)S(1)} %get-tuple-element.21), channel_id=1, replica_groups=mesh['z_far'=4,'z_near'=2,'y_far'=4,'y_near'=2,'x'=4,'core'=2] {'z_far',..., dimensions={0} | all-to-all | bytes 16384 | tf_op jit(solution)/shard_map/all_to_all | solution.py:266
  121.9 11.9 %all_to_all.39.got_ref = f32[32,1,128]{2,1,0:T(1,128)S(1)} all-to-all(f32[32,1,128]{2,1,0:T(1,128)S(1)} %shard_map.55), channel_id=1, replica_groups=mesh['z_far'=4,'z_near'=2,'y_far'=4,'y_near'=2,'x'=4,'core'=2] {'y_far',..., dimensions={0} | all-to-all | bytes 32768 | tf_op jit(solution)/shard_map/all_to_all | solution.py:266
  133.7 0.7 shard_map.56
  (1 shorter events, 0.0 us)
Async XLA Ops:
  0.6 0.8 copy-start
  1.4 0.7 copy-start.2
  2.1 67.1 %copy-start.1 = (f32[96,64]{0,1:T(8,128)S(1)}, f32[96,64]{0,1:T(8,128)}, u32[]{:S(2)}) copy-start(f32[96,64]{0,1:T(8,128)} %param.3) | copy-start | bytes 73732
  3.0 33.3 %all-to-all-start = ((f32[16,56,128]{2,1,0:T(8,128)}), f32[16,56,128]{2,1,0:T(8,128)S(1)}, u32[]{:S(2)}, u32[]{:S(2)}) async-start(f32[16,56,128]{2,1,0:T(8,128)} %get-tuple-element.14), calls=%async_computation | async-start | bytes 917504 | tf_op jit(solution)/shard_map/all_to_all | solution.py:266
  36.3 11.2 %all-to-all-start.1 = ((f32[16,8,128]{2,1,0:T(8,128)}), f32[16,8,128]{2,1,0:T(8,128)S(1)}, u32[]{:S(2)}, u32[]{:S(2)}) async-start(f32[16,8,128]{2,1,0:T(8,128)} %get-tuple-element.15), calls=%async_computation.1 | async-start | bytes 131072 | tf_op jit(solution)/shard_map/all_to_all | solution.py:266

commit v7 on v6

--- a/solution.py
+++ b/solution.py
@@ -2,6 +2,7 @@
 
 import jax
 import jax.numpy as jnp
+import numpy as np
 from jax import lax
 from jax.experimental import pallas as pl
 from jax.experimental.pallas import tpu as pltpu
@@ -19,10 +20,10 @@
 BF16 = jnp.bfloat16
 F32 = jnp.float32
 AXES = {"z_far": 4, "z_near": 2, "y_far": 4, "y_near": 2, "x": 4, "core": 2}
-FAR, FAR_SIZE = ("z_far", "y_far"), 16
-MID, MID_SIZE = ("z_near", "y_near", "x"), 16
-FIRST, FIRST_SIZE = ("z_far", "z_near", "core"), 16
-LAST, LAST_SIZE = ("y_far", "y_near", "x"), 32
+FAR, FAR_SIZE = {"z_far": 2, "y_far": 2}, 16
+MID, MID_SIZE = {"z_near": 0, "y_near": 0, "x": 2}, 16
+FIRST, FIRST_SIZE = {"z_far": 2, "z_near": 0, "core": 0}, 16
+LAST, LAST_SIZE = {"y_far": 2, "y_near": 0, "x": 2}, 32
 GATHERED = 2 * FAR_SIZE
 ROWS, COLS = MID_SIZE * MICS, GATHERED * MICS
 SINC = (
@@ -34,6 +35,16 @@
     -1.9848603010177612,
 )
 PARAMS = pltpu.CompilerParams(vmem_limit_bytes=24 * 1024 * 1024)
+
+
+def groups_of(axes):
+    places = np.arange(math.prod(AXES.values())).reshape(tuple(AXES.values()))
+    names = list(AXES)
+    for name, first in axes.items():
+        places = np.roll(places, -first, names.index(name))
+    members = math.prod(AXES[name] for name in axes)
+    places = np.moveaxis(places, [names.index(name) for name in axes], range(-len(axes), 0))
+    return places.reshape(-1, members).tolist()
 
 
 def dot(left, right):
@@ -262,8 +273,9 @@
     field = right_side.T
     block = (MICS, LANES)
 
-    def exchange(value, axis):
-        return lax.all_to_all(value, axis, 0, 0)
+    def exchange(value, axes):
+        groups = groups_of(axes)
+        return lax.all_to_all(value, tuple(AXES), 0, 0, axis_index_groups=groups)
 
     def gather(value):
         both = lax.all_gather(exchange(value, FAR), "core")

time: 135 us -> 126 us (0.933)
  waiting for transfers between devices: 18 us -> 10.3 us
  blocking collectives: 78.6 us -> 73.2 us
  starting transfers between devices: 21.2 us -> 25 us
    all_to_all x2, waiting for transfers between devices: 18 us -> 10.3 us  [exchange(): return lax.all_to_all(value, tuple(AXES), 0, 0, axis_index_groups=groups)]
    all_to_all x5, blocking collectives: 67.7 us -> 63.2 us  [exchange(): return lax.all_to_all(value, tuple(AXES), 0, 0, axis_index_groups=groups)]
    all_to_all x2, starting transfers between devices: 21.2 us -> 25 us  [exchange(): return lax.all_to_all(value, tuple(AXES), 0, 0, axis_index_groups=groups)]
  transfers between devices with their start and end apart: 2 -> 2, of which waited for: 2 -> 1; matrix products, arithmetic and copies ran while one was open for 0% -> 0% of each run, Pallas kernels for 0% -> 0%
where the time goes in v7:
time: 126 us; the launch traced here: 125 us
  blocking collectives  73.2 us (58%)
  starting transfers between devices  25 us (20%)
  Pallas kernels  13.9 us (11%)
  waiting for transfers between devices  10.3 us (8%)
  local copies, waits for them, and re-layouts  1.44 us (1%)
  between operations  1.31 us (1%)
    all_to_all x5, blocking collectives, exchange(): return lax.all_to_all(value, tuple(AXES), 0, 0, axis_index_groups=groups)  63.2 us
    all_to_all x2, starting transfers between devices, exchange(): return lax.all_to_all(value, tuple(AXES), 0, 0, axis_index_groups=groups)  25 us
    all_to_all x2, waiting for transfers between devices, exchange(): return lax.all_to_all(value, tuple(AXES), 0, 0, axis_index_groups=groups)  10.3 us
    all_gather x2, blocking collectives, gather(): both = lax.all_gather(exchange(value, FAR), 'core')  10 us
    pallas_call x1, Pallas kernels, local(): call(first_kernel, [((MID_SIZE, PACKED, LANES), F32), ((ROWS, COLS), BF16...  8.97 us
    pallas_call x1, Pallas kernels, local(): call(second_kernel, [((MID_SIZE, PACKED + EXTRA, LANES), F32)], scratch_s...  2.92 us
  transfers between devices with their start and end apart: 2, of which 1 were waited for; matrix products, arithmetic and copies ran while one was open for 0% of the time, Pallas kernels for 0%

profile of v7, /device:TPU:1, one launch (start us, length us, event | category | flops | bytes accessed | tf_op | source)
XLA Modules:
  0.0 125.1 jit_solution(17898451038416590903)
XLA Ops:
  0.6 0.0 copy-start
  0.6 0.7 copy-done
  1.4 0.0 copy-start.2
  1.4 0.7 copy-done.2
  2.1 0.0 copy-start.1
  2.1 0.9 shard_map.50
  3.0 18.4 %all-to-all-start = ((f32[16,56,128]{2,1,0:T(8,128)}), f32[16,56,128]{2,1,0:T(8,128)S(1)}, u32[]{:S(2)}, u32[]{:S(2)}) async-start(f32[16,56,128]{2,1,0:T(8,128)} %get-tuple-element.14), calls=%async_computation | async-start | bytes 917504 | tf_op jit(solution)/shard_map/all_to_all | solution.py:278
  22.1 10.3 %all-to-all-done = f32[16,56,128]{2,1,0:T(8,128)S(1)} async-done(((f32[16,56,128]{2,1,0:T(8,128)}), f32[16,56,128]{2,1,0:T(8,128)S(1)}, u32[]{:S(2)}, u32[]{:S(2)}) %all-to-all-start) | async-done | bytes 458784 | tf_op jit(solution)/shard_map/all_to_all | solution.py:278
  32.4 6.5 %all-to-all-start.1 = ((f32[16,8,128]{2,1,0:T(8,128)}), f32[16,8,128]{2,1,0:T(8,128)S(1)}, u32[]{:S(2)}, u32[]{:S(2)}) async-start(f32[16,8,128]{2,1,0:T(8,128)} %get-tuple-element.15), calls=%async_computation.1 | async-start | bytes 131072 | tf_op jit(solution)/shard_map/all_to_all | solution.py:278
  38.9 3.9 %all-gather.col_ref = f32[32,56,128]{2,1,0:T(8,128)S(1)} all-gather(f32[16,56,128]{2,1,0:T(8,128)S(1)} %all-to-all-done), channel_id=2, replica_groups=mesh['z_far'=4,'z_near'=2,'y_far'=4,'y_near'=2,'x'=4,'core'=2] {'core'}, dimensions={0}, use_global_device_ids=true | all-gather | bytes 1376256 | tf_op jit(solution)/shard_map/all_gather | solution.py:281
  42.8 0.0 all-to-all-done.1.row_ref
  42.8 9.0 %shard_map.51 = (f32[16,48,128]{2,1,0:T(8,128)S(1)}, bf16[1024,2048]{1,0:T(8,128)(2,1)S(1)}, bf16[1024,2048]{1,0:T(8,128)(2,1)S(1)}) custom-call(f32[32,56,128]{2,1,0:T(8,128)S(1)} %all-gather.col_ref, f32[16,8,128]{2,1,0:T(8,128)S(1)} %all-to-all-done.1.row_ref, f32[1]{0:T(128)S(6)} %copy.5.wave_ref), custom_call_target="tpu_custom_call" | custom-call | tf_op jit(solution)/shard_map/pallas_call | solution.py:293
  51.8 10.8 %all_to_all.35.got_ref = f32[16,48,128]{2,1,0:T(8,128)S(1)} all-to-all(f32[16,48,128]{2,1,0:T(8,128)S(1)} %get-tuple-element.16), channel_id=1, replica_groups={{4,6,0,2,12,14,8,10,68,70,64,66,76,78,72,74},{5,7,1,3,13,15,9,11,69,71,..., dimensions={0} | all-to-all | bytes 786432 | tf_op jit(solution)/shard_map/all_to_all | solution.py:278
  62.6 0.0 copy-done.1
  62.6 0.2 shard_map.52
  62.9 17.6 %all_to_all.36 = f32[16,48,128]{2,1,0:T(8,128)S(1)} all-to-all(f32[16,48,128]{2,1,0:T(8,128)S(1)} %get-tuple-element.17), channel_id=1, replica_groups={{288,304,256,272,416,432,384,400,32,48,0,16,160,176,128,144},{289,305,2..., dimensions={0} | all-to-all | bytes 786432 | tf_op jit(solution)/shard_map/all_to_all | solution.py:278
  80.4 6.1 %all-gather.1.got_ref = f32[32,48,128]{2,1,0:T(8,128)S(1)} all-gather(f32[16,48,128]{2,1,0:T(8,128)S(1)} %all_to_all.36), channel_id=3, replica_groups=mesh['z_far'=4,'z_near'=2,'y_far'=4,'y_near'=2,'x'=4,'core'=2] {'core'}, dimensions={0}, use_global_device_ids=true | all-gather | bytes 1179648 | tf_op jit(solution)/shard_map/all_gather | solution.py:281
  86.5 2.9 %shard_map.53 = f32[16,56,128]{2,1,0:T(8,128)S(1)} custom-call(f32[32,48,128]{2,1,0:T(8,128)S(1)} %all-gather.1.got_ref, f32[32,56,128]{2,1,0:T(8,128)S(1)} %all-gather.col_ref, bf16[1024,2048]{1,0:T(8,128)(2,1)S(1)} %get-tuple-element.18.high_ref, bf16[1024,2048]{1,0:T(8,128)(2,1)S(1)} %get-tuple-element.19.low_ref), custom_call_target="tpu_custom_call" | custom-call | tf_op jit(solution)/shard_map/pallas_call | solution.py:306
  89.5 13.4 %all_to_all.37.got_ref = f32[16,56,128]{2,1,0:T(8,128)S(1)} all-to-all(f32[16,56,128]{2,1,0:T(8,128)S(1)} %shard_map.53), channel_id=1, replica_groups={{4,6,0,2,12,14,8,10,68,70,64,66,76,78,72,74},{5,7,1,3,13,15,9,11,69,71,..., dimensions={0} | all-to-all | bytes 917504 | tf_op jit(solution)/shard_map/all_to_all | solution.py:278
  102.9 0.1 shard_map.54
  103.0 10.7 %all_to_all.38.got_ref = f32[16,1,128]{2,1,0:T(1,128)S(1)} all-to-all(f32[16,1,128]{2,1,0:T(1,128)S(1)} %get-tuple-element.21), channel_id=1, replica_groups={{256,257,320,321,384,385,448,449,0,1,64,65,128,129,192,193},{258,259,32..., dimensions={0} | all-to-all | bytes 16384 | tf_op jit(solution)/shard_map/all_to_all | solution.py:278
  113.7 10.7 %all_to_all.39.got_ref = f32[32,1,128]{2,1,0:T(1,128)S(1)} all-to-all(f32[32,1,128]{2,1,0:T(1,128)S(1)} %shard_map.55), channel_id=1, replica_groups={{36,38,32,34,44,46,40,42,52,54,48,50,60,62,56,58,4,6,0,2,12,14,8,10,20,..., dimensions={0} | all-to-all | bytes 32768 | tf_op jit(solution)/shard_map/all_to_all | solution.py:278
  124.4 0.7 shard_map.56
  (1 shorter events, 0.0 us)
Async XLA Ops:
  0.6 0.8 copy-start
  1.4 0.7 copy-start.2
  2.1 60.5 %copy-start.1 = (f32[96,64]{0,1:T(8,128)S(1)}, f32[96,64]{0,1:T(8,128)}, u32[]{:S(2)}) copy-start(f32[96,64]{0,1:T(8,128)} %param.3) | copy-start | bytes 73732
  3.0 29.4 %all-to-all-start = ((f32[16,56,128]{2,1,0:T(8,128)}), f32[16,56,128]{2,1,0:T(8,128)S(1)}, u32[]{:S(2)}, u32[]{:S(2)}) async-start(f32[16,56,128]{2,1,0:T(8,128)} %get-tuple-element.14), calls=%async_computation | async-start | bytes 917504 | tf_op jit(solution)/shard_map/all_to_all | solution.py:278
  32.4 10.4 %all-to-all-start.1 = ((f32[16,8,128]{2,1,0:T(8,128)}), f32[16,8,128]{2,1,0:T(8,128)S(1)}, u32[]{:S(2)}, u32[]{:S(2)}) async-start(f32[16,8,128]{2,1,0:T(8,128)} %get-tuple-element.15), calls=%async_computation.1 | async-start | bytes 131072 | tf_op jit(solution)/shard_map/all_to_all | solution.py:278

commit v8 on v7

--- a/solution.py
+++ b/solution.py
@@ -89,11 +89,9 @@
     return jnp.sum(value, axis=0, keepdims=True)
 
 
-def start_kernel(field_ref, points_ref, col_ref, row_ref):
-    points = points_ref[...]
-    points = jnp.concatenate([points, jnp.zeros((EXTRA - 3, MICS), F32)], axis=0)
-    points = widen(points)
-    block = jnp.concatenate([pack(field_ref[...]), points], axis=0)
+def start_kernel(both_ref, col_ref, row_ref):
+    points = both_ref[MICS:]
+    block = jnp.concatenate([pack(both_ref[:MICS]), points], axis=0)
     col_ref[...] = jnp.broadcast_to(block[None], col_ref.shape)
     row_ref[...] = jnp.broadcast_to(points[None], row_ref.shape)
 
@@ -153,18 +151,21 @@
         out_ref[index * (STEP // MICS) + i, :PACKED, :] = packed
 
 
-def first_kernel(
-    col_ref, row_ref, wave_ref, out_ref, high_ref, low_ref, weights_ref, col_f, row_f
-):
-    wave = wave_ref[0]
-
+def prepare_kernel(col_ref, wave_ref, weights_ref, col_f):
     def place(index, carry):
         put_weights(weights_ref, index, unpack(col_ref[index, :PACKED, :]))
         return carry
 
     lax.fori_loop(0, GATHERED, place, 0, unroll=True)
-    col_f[...] = factors(points_of(col_ref, GATHERED, PACKED), wave, False).astype(BF16)
-    row_f[...] = factors(points_of(row_ref, MID_SIZE, 0), wave, True).T.astype(BF16)
+    cols = points_of(col_ref, GATHERED, PACKED)
+    col_f[...] = factors(cols, wave_ref[0], False).astype(BF16)
+
+
+def first_kernel(
+    weights_ref, col_f, row_ref, wave_ref, out_ref, high_ref, low_ref, row_f
+):
+    rows = points_of(row_ref, MID_SIZE, 0)
+    row_f[...] = factors(rows, wave_ref[0], True).T.astype(BF16)
 
     def some_rows(index, carry):
         at = pl.ds(pl.multiple_of(index * STEP, STEP), STEP)
@@ -283,23 +284,25 @@
 
     scalar = pl.BlockSpec(memory_space=pltpu.SMEM)
     vector = pl.BlockSpec(memory_space=pltpu.VMEM)
+    spare = jnp.pad(positions, ((0, EXTRA - 3), (0, LANES - MICS)))
     to_cols, points = call(
         start_kernel,
         [((FAR_SIZE, PACKED + EXTRA, LANES), F32), ((MID_SIZE, EXTRA, LANES), F32)],
-    )(field, positions)
+    )(jnp.concatenate([widen(field), spare], axis=0))
     col_blocks = gather(to_cols)
     row_points = exchange(points, MID)
 
+    weights, col_factors = call(
+        prepare_kernel,
+        [((COLS, 2 * LANES), BF16), ((DEPTH, COLS), BF16)],
+        in_specs=[vector, scalar],
+    )(col_blocks, wavenumber)
     partial, high, low = call(
         first_kernel,
         [((MID_SIZE, PACKED, LANES), F32), ((ROWS, COLS), BF16), ((ROWS, COLS), BF16)],
-        in_specs=[vector, vector, scalar],
-        scratch_shapes=[
-            pltpu.VMEM((COLS, 2 * LANES), BF16),
-            pltpu.VMEM((DEPTH, COLS), BF16),
-            pltpu.VMEM((ROWS, DEPTH), BF16),
-        ],
-    )(col_blocks, row_points, wavenumber)
+        in_specs=[vector, vector, vector, scalar],
+        scratch_shapes=[pltpu.VMEM((ROWS, DEPTH), BF16)],
+    )(weights, col_factors, row_points, wavenumber)
     image, to_cols = call(image_kernel, [(block, F32), ((FAR_SIZE, PACKED, LANES), F32)])(
         exchange(partial, MID), field
     )

time: 126 us -> 126 us (level)
  local copies, waits for them, and re-layouts: 1.44 us -> 0.01 us
    all_to_all x5, blocking collectives: 63.2 us -> 65 us  [exchange(): return lax.all_to_all(value, tuple(AXES), 0, 0, axis_index_groups=groups)]
    all_gather x2, blocking collectives: 10 us -> 8.5 us  [gather(): both = lax.all_gather(exchange(value, FAR), 'core')]
    unnamed x6 -> x2, local copies, waits for them, and re-layouts: 1.44 us -> 0.01 us
where the time goes in v8:
time: 126 us; the launch traced here: 125 us
  blocking collectives  73.5 us (58%)
  starting transfers between devices  25 us (20%)
  Pallas kernels  14.1 us (11%)
  waiting for transfers between devices  10.3 us (8%)
  between operations  1.32 us (1%)
    all_to_all x5, blocking collectives, exchange(): return lax.all_to_all(value, tuple(AXES), 0, 0, axis_index_groups=groups)  65 us
    all_to_all x2, starting transfers between devices, exchange(): return lax.all_to_all(value, tuple(AXES), 0, 0, axis_index_groups=groups)  25 us
    all_to_all x2, waiting for transfers between devices, exchange(): return lax.all_to_all(value, tuple(AXES), 0, 0, axis_index_groups=groups)  10.3 us
    pallas_call x1, Pallas kernels, local(): call(first_kernel, [((MID_SIZE, PACKED, LANES), F32), ((ROWS, COLS), BF16...  8.88 us
    all_gather x2, blocking collectives, gather(): both = lax.all_gather(exchange(value, FAR), 'core')  8.5 us
    pallas_call x1, Pallas kernels, local(): call(second_kernel, [((MID_SIZE, PACKED + EXTRA, LANES), F32)], scratch_s...  2.93 us
  transfers between devices with their start and end apart: 2, of which 1 were waited for; matrix products, arithmetic and copies ran while one was open for 0% of the time, Pallas kernels for 0%

profile of v8, /device:TPU:1, one launch (start us, length us, event | category | flops | bytes accessed | tf_op | source)
XLA Modules:
  0.0 125.0 jit_solution(4942021232992215516)
XLA Ops:
  0.6 0.0 copy-start
  0.6 0.8 select_maximum_fusion.both_ref
  1.5 0.9 shard_map.50
  2.4 18.4 %all-to-all-start = ((f32[16,56,128]{2,1,0:T(8,128)}), f32[16,56,128]{2,1,0:T(8,128)S(1)}, u32[]{:S(2)}, u32[]{:S(2)}) async-start(f32[16,56,128]{2,1,0:T(8,128)} %get-tuple-element.16), calls=%async_computation | async-start | bytes 917504 | tf_op jit(solution)/shard_map/all_to_all | solution.py:279
  21.5 10.3 %all-to-all-done = f32[16,56,128]{2,1,0:T(8,128)S(1)} async-done(((f32[16,56,128]{2,1,0:T(8,128)}), f32[16,56,128]{2,1,0:T(8,128)S(1)}, u32[]{:S(2)}, u32[]{:S(2)}) %all-to-all-start) | async-done | bytes 458784 | tf_op jit(solution)/shard_map/all_to_all | solution.py:279
  31.8 6.5 %all-to-all-start.1 = ((f32[16,8,128]{2,1,0:T(8,128)}), f32[16,8,128]{2,1,0:T(8,128)S(1)}, u32[]{:S(2)}, u32[]{:S(2)}) async-start(f32[16,8,128]{2,1,0:T(8,128)} %get-tuple-element.19), calls=%async_computation.1 | async-start | bytes 131072 | tf_op jit(solution)/shard_map/all_to_all | solution.py:279
  38.3 3.9 %all-gather.col_ref = f32[32,56,128]{2,1,0:T(8,128)S(1)} all-gather(f32[16,56,128]{2,1,0:T(8,128)S(1)} %all-to-all-done), channel_id=2, replica_groups=mesh['z_far'=4,'z_near'=2,'y_far'=4,'y_near'=2,'x'=4,'core'=2] {'core'}, dimensions={0}, use_global_device_ids=true | all-gather | bytes 1376256 | tf_op jit(solution)/shard_map/all_gather | solution.py:282
  42.2 0.3 shard_map.51
  42.5 0.0 all-to-all-done.1.row_ref
  42.5 8.9 %shard_map.52 = (f32[16,48,128]{2,1,0:T(8,128)S(1)}, bf16[1024,2048]{1,0:T(8,128)(2,1)S(1)}, bf16[1024,2048]{1,0:T(8,128)(2,1)S(1)}) custom-call(bf16[2048,256]{1,0:T(8,128)(2,1)S(1)} %get-tuple-element.17.weights_ref, bf16[64,2048]{1,0:T(8,128)(2,1)S(1)} %get-tuple-element.18.col_f, f32[16,8,128]{2,1,0:T(8,128)S(1)} %all-to-all-done.1.row_ref, ...), custom_call_target="tpu_custom_call" | custom-call | tf_op jit(solution)/shard_map/pallas_call | solution.py:300
  51.4 10.9 %all_to_all.35.got_ref = f32[16,48,128]{2,1,0:T(8,128)S(1)} all-to-all(f32[16,48,128]{2,1,0:T(8,128)S(1)} %get-tuple-element.20), channel_id=1, replica_groups={{4,6,0,2,12,14,8,10,68,70,64,66,76,78,72,74},{5,7,1,3,13,15,9,11,69,71,..., dimensions={0} | all-to-all | bytes 786432 | tf_op jit(solution)/shard_map/all_to_all | solution.py:279
  62.3 0.0 copy-done
  62.3 0.2 shard_map.53
  62.6 19.4 %all_to_all.36 = f32[16,48,128]{2,1,0:T(8,128)S(1)} all-to-all(f32[16,48,128]{2,1,0:T(8,128)S(1)} %get-tuple-element.21), channel_id=1, replica_groups={{288,304,256,272,416,432,384,400,32,48,0,16,160,176,128,144},{289,305,2..., dimensions={0} | all-to-all | bytes 786432 | tf_op jit(solution)/shard_map/all_to_all | solution.py:279
  81.9 4.6 %all-gather.1.got_ref = f32[32,48,128]{2,1,0:T(8,128)S(1)} all-gather(f32[16,48,128]{2,1,0:T(8,128)S(1)} %all_to_all.36), channel_id=3, replica_groups=mesh['z_far'=4,'z_near'=2,'y_far'=4,'y_near'=2,'x'=4,'core'=2] {'core'}, dimensions={0}, use_global_device_ids=true | all-gather | bytes 1179648 | tf_op jit(solution)/shard_map/all_gather | solution.py:282
  86.5 2.9 %shard_map.54 = f32[16,56,128]{2,1,0:T(8,128)S(1)} custom-call(f32[32,48,128]{2,1,0:T(8,128)S(1)} %all-gather.1.got_ref, f32[32,56,128]{2,1,0:T(8,128)S(1)} %all-gather.col_ref, bf16[1024,2048]{1,0:T(8,128)(2,1)S(1)} %get-tuple-element.22.high_ref, bf16[1024,2048]{1,0:T(8,128)(2,1)S(1)} %get-tuple-element.23.low_ref), custom_call_target="tpu_custom_call" | custom-call | tf_op jit(solution)/shard_map/pallas_call | solution.py:309
  89.4 13.2 %all_to_all.37.got_ref = f32[16,56,128]{2,1,0:T(8,128)S(1)} all-to-all(f32[16,56,128]{2,1,0:T(8,128)S(1)} %shard_map.54), channel_id=1, replica_groups={{4,6,0,2,12,14,8,10,68,70,64,66,76,78,72,74},{5,7,1,3,13,15,9,11,69,71,..., dimensions={0} | all-to-all | bytes 917504 | tf_op jit(solution)/shard_map/all_to_all | solution.py:279
  102.6 0.1 shard_map.55
  102.8 10.9 %all_to_all.38.got_ref = f32[16,1,128]{2,1,0:T(1,128)S(1)} all-to-all(f32[16,1,128]{2,1,0:T(1,128)S(1)} %get-tuple-element.25), channel_id=1, replica_groups={{256,257,320,321,384,385,448,449,0,1,64,65,128,129,192,193},{258,259,32..., dimensions={0} | all-to-all | bytes 16384 | tf_op jit(solution)/shard_map/all_to_all | solution.py:279
  113.6 10.7 %all_to_all.39.got_ref = f32[32,1,128]{2,1,0:T(1,128)S(1)} all-to-all(f32[32,1,128]{2,1,0:T(1,128)S(1)} %shard_map.56), channel_id=1, replica_groups={{36,38,32,34,44,46,40,42,52,54,48,50,60,62,56,58,4,6,0,2,12,14,8,10,20,..., dimensions={0} | all-to-all | bytes 32768 | tf_op jit(solution)/shard_map/all_to_all | solution.py:279
  124.4 0.7 shard_map.57
  (1 shorter events, 0.0 us)
Async XLA Ops:
  0.6 61.7 %copy-start = (f32[96,64]{0,1:T(8,128)S(1)}, f32[96,64]{0,1:T(8,128)}, u32[]{:S(2)}) copy-start(f32[96,64]{0,1:T(8,128)} %param.3) | copy-start | bytes 73732
  2.4 29.4 %all-to-all-start = ((f32[16,56,128]{2,1,0:T(8,128)}), f32[16,56,128]{2,1,0:T(8,128)S(1)}, u32[]{:S(2)}, u32[]{:S(2)}) async-start(f32[16,56,128]{2,1,0:T(8,128)} %get-tuple-element.16), calls=%async_computation | async-start | bytes 917504 | tf_op jit(solution)/shard_map/all_to_all | solution.py:279
  31.8 10.8 %all-to-all-start.1 = ((f32[16,8,128]{2,1,0:T(8,128)}), f32[16,8,128]{2,1,0:T(8,128)S(1)}, u32[]{:S(2)}, u32[]{:S(2)}) async-start(f32[16,8,128]{2,1,0:T(8,128)} %get-tuple-element.19), calls=%async_computation.1 | async-start | bytes 131072 | tf_op jit(solution)/shard_map/all_to_all | solution.py:279

commit v9 on v8

--- a/solution.py
+++ b/solution.py
@@ -14,15 +14,15 @@
 FRAMES = 96
 PACKED = 48
 EXTRA = 8
-STEP = 256
+STEP = 512
 DEPTH = 64
 SHIFT = 0.01
 BF16 = jnp.bfloat16
 F32 = jnp.float32
 AXES = {"z_far": 4, "z_near": 2, "y_far": 4, "y_near": 2, "x": 4, "core": 2}
 FAR, FAR_SIZE = {"z_far": 2, "y_far": 2}, 16
-MID, MID_SIZE = {"z_near": 0, "y_near": 0, "x": 2}, 16
-FIRST, FIRST_SIZE = {"z_far": 2, "z_near": 0, "core": 0}, 16
+MID, MID_SIZE = {"z_near": 1, "y_near": 1, "x": 2}, 16
+FIRST, FIRST_SIZE = {"z_far": 2, "z_near": 0, "core": 1}, 16
 LAST, LAST_SIZE = {"y_far": 2, "y_near": 0, "x": 2}, 32
 GATHERED = 2 * FAR_SIZE
 ROWS, COLS = MID_SIZE * MICS, GATHERED * MICS

time: 126 us -> 125 us (level)
  blocking collectives: 73.5 us -> 71.4 us
    all_to_all x5, blocking collectives: 65 us -> 62.3 us  [exchange(): return lax.all_to_all(value, tuple(AXES), 0, 0, axis_index_groups=groups)]
where the time goes in v9:
time: 125 us; the launch traced here: 124 us
  blocking collectives  71.4 us (57%)
  starting transfers between devices  26.1 us (21%)
  Pallas kernels  14 us (11%)
  waiting for transfers between devices  10.3 us (8%)
  between operations  1.32 us (1%)
    all_to_all x5, blocking collectives, exchange(): return lax.all_to_all(value, tuple(AXES), 0, 0, axis_index_groups=groups)  62.3 us
    all_to_all x2, starting transfers between devices, exchange(): return lax.all_to_all(value, tuple(AXES), 0, 0, axis_index_groups=groups)  26.1 us
    all_to_all x2, waiting for transfers between devices, exchange(): return lax.all_to_all(value, tuple(AXES), 0, 0, axis_index_groups=groups)  10.3 us
    all_gather x2, blocking collectives, gather(): both = lax.all_gather(exchange(value, FAR), 'core')  9.12 us
    pallas_call x1, Pallas kernels, local(): call(first_kernel, [((MID_SIZE, PACKED, LANES), F32), ((ROWS, COLS), BF16...  8.78 us
    pallas_call x1, Pallas kernels, local(): call(second_kernel, [((MID_SIZE, PACKED + EXTRA, LANES), F32)], scratch_s...  2.88 us
  transfers between devices with their start and end apart: 2, of which 1 were waited for; matrix products, arithmetic and copies ran while one was open for 0% of the time, Pallas kernels for 0%

profile of v9, /device:TPU:1, one launch (start us, length us, event | category | flops | bytes accessed | tf_op | source)
XLA Modules:
  0.0 124.0 jit_solution(4331530014317751886)
XLA Ops:
  0.6 0.0 copy-start
  0.6 0.8 select_maximum_fusion.both_ref
  1.5 0.9 shard_map.50
  2.4 18.4 %all-to-all-start = ((f32[16,56,128]{2,1,0:T(8,128)}), f32[16,56,128]{2,1,0:T(8,128)S(1)}, u32[]{:S(2)}, u32[]{:S(2)}) async-start(f32[16,56,128]{2,1,0:T(8,128)} %get-tuple-element.16), calls=%async_computation | async-start | bytes 917504 | tf_op jit(solution)/shard_map/all_to_all | solution.py:279
  21.5 10.3 %all-to-all-done = f32[16,56,128]{2,1,0:T(8,128)S(1)} async-done(((f32[16,56,128]{2,1,0:T(8,128)}), f32[16,56,128]{2,1,0:T(8,128)S(1)}, u32[]{:S(2)}, u32[]{:S(2)}) %all-to-all-start) | async-done | bytes 458784 | tf_op jit(solution)/shard_map/all_to_all | solution.py:279
  31.8 7.7 %all-to-all-start.1 = ((f32[16,8,128]{2,1,0:T(8,128)}), f32[16,8,128]{2,1,0:T(8,128)S(1)}, u32[]{:S(2)}, u32[]{:S(2)}) async-start(f32[16,8,128]{2,1,0:T(8,128)} %get-tuple-element.19), calls=%async_computation.1 | async-start | bytes 131072 | tf_op jit(solution)/shard_map/all_to_all | solution.py:279
  39.5 3.6 %all-gather.col_ref = f32[32,56,128]{2,1,0:T(8,128)S(1)} all-gather(f32[16,56,128]{2,1,0:T(8,128)S(1)} %all-to-all-done), channel_id=2, replica_groups=mesh['z_far'=4,'z_near'=2,'y_far'=4,'y_near'=2,'x'=4,'core'=2] {'core'}, dimensions={0}, use_global_device_ids=true | all-gather | bytes 1376256 | tf_op jit(solution)/shard_map/all_gather | solution.py:282
  43.1 0.3 shard_map.51
  43.4 0.0 all-to-all-done.1.row_ref
  43.4 8.8 %shard_map.52 = (f32[16,48,128]{2,1,0:T(8,128)S(1)}, bf16[1024,2048]{1,0:T(8,128)(2,1)S(1)}, bf16[1024,2048]{1,0:T(8,128)(2,1)S(1)}) custom-call(bf16[2048,256]{1,0:T(8,128)(2,1)S(1)} %get-tuple-element.17.weights_ref, bf16[64,2048]{1,0:T(8,128)(2,1)S(1)} %get-tuple-element.18.col_f, f32[16,8,128]{2,1,0:T(8,128)S(1)} %all-to-all-done.1.row_ref, ...), custom_call_target="tpu_custom_call" | custom-call | tf_op jit(solution)/shard_map/pallas_call | solution.py:300
  52.2 9.8 %all_to_all.35.got_ref = f32[16,48,128]{2,1,0:T(8,128)S(1)} all-to-all(f32[16,48,128]{2,1,0:T(8,128)S(1)} %get-tuple-element.20), channel_id=1, replica_groups={{76,78,72,74,68,70,64,66,12,14,8,10,4,6,0,2},{77,79,73,75,69,71,65,67,1..., dimensions={0} | all-to-all | bytes 786432 | tf_op jit(solution)/shard_map/all_to_all | solution.py:279
  62.0 0.0 copy-done
  62.0 0.2 shard_map.53
  62.2 18.5 %all_to_all.36 = f32[16,48,128]{2,1,0:T(8,128)S(1)} all-to-all(f32[16,48,128]{2,1,0:T(8,128)S(1)} %get-tuple-element.21), channel_id=1, replica_groups={{288,304,256,272,416,432,384,400,32,48,0,16,160,176,128,144},{289,305,2..., dimensions={0} | all-to-all | bytes 786432 | tf_op jit(solution)/shard_map/all_to_all | solution.py:279
  80.7 5.5 %all-gather.1.got_ref = f32[32,48,128]{2,1,0:T(8,128)S(1)} all-gather(f32[16,48,128]{2,1,0:T(8,128)S(1)} %all_to_all.36), channel_id=3, replica_groups=mesh['z_far'=4,'z_near'=2,'y_far'=4,'y_near'=2,'x'=4,'core'=2] {'core'}, dimensions={0}, use_global_device_ids=true | all-gather | bytes 1179648 | tf_op jit(solution)/shard_map/all_gather | solution.py:282
  86.2 2.9 %shard_map.54 = f32[16,56,128]{2,1,0:T(8,128)S(1)} custom-call(f32[32,48,128]{2,1,0:T(8,128)S(1)} %all-gather.1.got_ref, f32[32,56,128]{2,1,0:T(8,128)S(1)} %all-gather.col_ref, bf16[1024,2048]{1,0:T(8,128)(2,1)S(1)} %get-tuple-element.22.high_ref, bf16[1024,2048]{1,0:T(8,128)(2,1)S(1)} %get-tuple-element.23.low_ref), custom_call_target="tpu_custom_call" | custom-call | tf_op jit(solution)/shard_map/pallas_call | solution.py:309
  89.1 13.2 %all_to_all.37.got_ref = f32[16,56,128]{2,1,0:T(8,128)S(1)} all-to-all(f32[16,56,128]{2,1,0:T(8,128)S(1)} %shard_map.54), channel_id=1, replica_groups={{76,78,72,74,68,70,64,66,12,14,8,10,4,6,0,2},{77,79,73,75,69,71,65,67,1..., dimensions={0} | all-to-all | bytes 917504 | tf_op jit(solution)/shard_map/all_to_all | solution.py:279
  102.4 0.1 shard_map.55
  102.5 10.0 %all_to_all.38.got_ref = f32[16,1,128]{2,1,0:T(1,128)S(1)} all-to-all(f32[16,1,128]{2,1,0:T(1,128)S(1)} %get-tuple-element.25), channel_id=1, replica_groups={{257,256,321,320,385,384,449,448,1,0,65,64,129,128,193,192},{259,258,32..., dimensions={0} | all-to-all | bytes 16384 | tf_op jit(solution)/shard_map/all_to_all | solution.py:279
  112.5 10.8 %all_to_all.39.got_ref = f32[32,1,128]{2,1,0:T(1,128)S(1)} all-to-all(f32[32,1,128]{2,1,0:T(1,128)S(1)} %shard_map.56), channel_id=1, replica_groups={{36,38,32,34,44,46,40,42,52,54,48,50,60,62,56,58,4,6,0,2,12,14,8,10,20,..., dimensions={0} | all-to-all | bytes 32768 | tf_op jit(solution)/shard_map/all_to_all | solution.py:279
  123.3 0.7 shard_map.57
  (1 shorter events, 0.0 us)
Async XLA Ops:
  0.6 61.4 %copy-start = (f32[96,64]{0,1:T(8,128)S(1)}, f32[96,64]{0,1:T(8,128)}, u32[]{:S(2)}) copy-start(f32[96,64]{0,1:T(8,128)} %param.3) | copy-start | bytes 73732
  2.4 29.4 %all-to-all-start = ((f32[16,56,128]{2,1,0:T(8,128)}), f32[16,56,128]{2,1,0:T(8,128)S(1)}, u32[]{:S(2)}, u32[]{:S(2)}) async-start(f32[16,56,128]{2,1,0:T(8,128)} %get-tuple-element.16), calls=%async_computation | async-start | bytes 917504 | tf_op jit(solution)/shard_map/all_to_all | solution.py:279
  31.8 11.7 %all-to-all-start.1 = ((f32[16,8,128]{2,1,0:T(8,128)}), f32[16,8,128]{2,1,0:T(8,128)S(1)}, u32[]{:S(2)}, u32[]{:S(2)}) async-start(f32[16,8,128]{2,1,0:T(8,128)} %get-tuple-element.19), calls=%async_computation.1 | async-start | bytes 131072 | tf_op jit(solution)/shard_map/all_to_all | solution.py:279

commit v10 on v9

--- a/solution.py
+++ b/solution.py
@@ -14,7 +14,7 @@
 FRAMES = 96
 PACKED = 48
 EXTRA = 8
-STEP = 512
+STEP = 1024
 DEPTH = 64
 SHIFT = 0.01
 BF16 = jnp.bfloat16

time: 125 us -> 125 us (level)
  no operation moved by 1% of the time
where the time goes in v10:
time: 125 us; the launch traced here: 124 us
  blocking collectives  71.2 us (57%)
  starting transfers between devices  26.1 us (21%)
  Pallas kernels  14.1 us (11%)
  waiting for transfers between devices  10.3 us (8%)
  between operations  1.32 us (1%)
    all_to_all x5, blocking collectives, exchange(): return lax.all_to_all(value, tuple(AXES), 0, 0, axis_index_groups=groups)  62.3 us
    all_to_all x2, starting transfers between devices, exchange(): return lax.all_to_all(value, tuple(AXES), 0, 0, axis_index_groups=groups)  26.1 us
    all_to_all x2, waiting for transfers between devices, exchange(): return lax.all_to_all(value, tuple(AXES), 0, 0, axis_index_groups=groups)  10.3 us
    all_gather x2, blocking collectives, gather(): both = lax.all_gather(exchange(value, FAR), 'core')  8.92 us
    pallas_call x1, Pallas kernels, local(): call(first_kernel, [((MID_SIZE, PACKED, LANES), F32), ((ROWS, COLS), BF16...  8.91 us
    pallas_call x1, Pallas kernels, local(): call(second_kernel, [((MID_SIZE, PACKED + EXTRA, LANES), F32)], scratch_s...  2.86 us
  transfers between devices with their start and end apart: 2, of which 1 were waited for; matrix products, arithmetic and copies ran while one was open for 0% of the time, Pallas kernels for 0%

profile of v10, /device:TPU:1, one launch (start us, length us, event | category | flops | bytes accessed | tf_op | source)
XLA Modules:
  0.0 123.9 jit_solution(18377187582907492716)
XLA Ops:
  0.6 0.0 copy-start
  0.6 0.8 select_maximum_fusion.both_ref
  1.5 0.9 shard_map.50
  2.4 18.4 %all-to-all-start = ((f32[16,56,128]{2,1,0:T(8,128)}), f32[16,56,128]{2,1,0:T(8,128)S(1)}, u32[]{:S(2)}, u32[]{:S(2)}) async-start(f32[16,56,128]{2,1,0:T(8,128)} %get-tuple-element.16), calls=%async_computation | async-start | bytes 917504 | tf_op jit(solution)/shard_map/all_to_all | solution.py:279
  21.5 10.3 %all-to-all-done = f32[16,56,128]{2,1,0:T(8,128)S(1)} async-done(((f32[16,56,128]{2,1,0:T(8,128)}), f32[16,56,128]{2,1,0:T(8,128)S(1)}, u32[]{:S(2)}, u32[]{:S(2)}) %all-to-all-start) | async-done | bytes 458784 | tf_op jit(solution)/shard_map/all_to_all | solution.py:279
  31.8 7.7 %all-to-all-start.1 = ((f32[16,8,128]{2,1,0:T(8,128)}), f32[16,8,128]{2,1,0:T(8,128)S(1)}, u32[]{:S(2)}, u32[]{:S(2)}) async-start(f32[16,8,128]{2,1,0:T(8,128)} %get-tuple-element.19), calls=%async_computation.1 | async-start | bytes 131072 | tf_op jit(solution)/shard_map/all_to_all | solution.py:279
  39.5 3.6 %all-gather.col_ref = f32[32,56,128]{2,1,0:T(8,128)S(1)} all-gather(f32[16,56,128]{2,1,0:T(8,128)S(1)} %all-to-all-done), channel_id=2, replica_groups=mesh['z_far'=4,'z_near'=2,'y_far'=4,'y_near'=2,'x'=4,'core'=2] {'core'}, dimensions={0}, use_global_device_ids=true | all-gather | bytes 1376256 | tf_op jit(solution)/shard_map/all_gather | solution.py:282
  43.1 0.3 shard_map.51
  43.4 0.0 all-to-all-done.1.row_ref
  43.4 8.9 %shard_map.52 = (f32[16,48,128]{2,1,0:T(8,128)S(1)}, bf16[1024,2048]{1,0:T(8,128)(2,1)S(1)}, bf16[1024,2048]{1,0:T(8,128)(2,1)S(1)}) custom-call(bf16[2048,256]{1,0:T(8,128)(2,1)S(1)} %get-tuple-element.17.weights_ref, bf16[64,2048]{1,0:T(8,128)(2,1)S(1)} %get-tuple-element.18.col_f, f32[16,8,128]{2,1,0:T(8,128)S(1)} %all-to-all-done.1.row_ref, ...), custom_call_target="tpu_custom_call" | custom-call | tf_op jit(solution)/shard_map/pallas_call | solution.py:300
  52.3 10.0 %all_to_all.35.got_ref = f32[16,48,128]{2,1,0:T(8,128)S(1)} all-to-all(f32[16,48,128]{2,1,0:T(8,128)S(1)} %get-tuple-element.20), channel_id=1, replica_groups={{76,78,72,74,68,70,64,66,12,14,8,10,4,6,0,2},{77,79,73,75,69,71,65,67,1..., dimensions={0} | all-to-all | bytes 786432 | tf_op jit(solution)/shard_map/all_to_all | solution.py:279
  62.3 0.0 copy-done
  62.3 0.2 shard_map.53
  62.5 18.5 %all_to_all.36 = f32[16,48,128]{2,1,0:T(8,128)S(1)} all-to-all(f32[16,48,128]{2,1,0:T(8,128)S(1)} %get-tuple-element.21), channel_id=1, replica_groups={{288,304,256,272,416,432,384,400,32,48,0,16,160,176,128,144},{289,305,2..., dimensions={0} | all-to-all | bytes 786432 | tf_op jit(solution)/shard_map/all_to_all | solution.py:279
  81.1 5.3 %all-gather.1.got_ref = f32[32,48,128]{2,1,0:T(8,128)S(1)} all-gather(f32[16,48,128]{2,1,0:T(8,128)S(1)} %all_to_all.36), channel_id=3, replica_groups=mesh['z_far'=4,'z_near'=2,'y_far'=4,'y_near'=2,'x'=4,'core'=2] {'core'}, dimensions={0}, use_global_device_ids=true | all-gather | bytes 1179648 | tf_op jit(solution)/shard_map/all_gather | solution.py:282
  86.4 2.9 %shard_map.54 = f32[16,56,128]{2,1,0:T(8,128)S(1)} custom-call(f32[32,48,128]{2,1,0:T(8,128)S(1)} %all-gather.1.got_ref, f32[32,56,128]{2,1,0:T(8,128)S(1)} %all-gather.col_ref, bf16[1024,2048]{1,0:T(8,128)(2,1)S(1)} %get-tuple-element.22.high_ref, bf16[1024,2048]{1,0:T(8,128)(2,1)S(1)} %get-tuple-element.23.low_ref), custom_call_target="tpu_custom_call" | custom-call | tf_op jit(solution)/shard_map/pallas_call | solution.py:309
  89.2 13.2 %all_to_all.37.got_ref = f32[16,56,128]{2,1,0:T(8,128)S(1)} all-to-all(f32[16,56,128]{2,1,0:T(8,128)S(1)} %shard_map.54), channel_id=1, replica_groups={{76,78,72,74,68,70,64,66,12,14,8,10,4,6,0,2},{77,79,73,75,69,71,65,67,1..., dimensions={0} | all-to-all | bytes 917504 | tf_op jit(solution)/shard_map/all_to_all | solution.py:279
  102.5 0.1 shard_map.55
  102.6 10.0 %all_to_all.38.got_ref = f32[16,1,128]{2,1,0:T(1,128)S(1)} all-to-all(f32[16,1,128]{2,1,0:T(1,128)S(1)} %get-tuple-element.25), channel_id=1, replica_groups={{257,256,321,320,385,384,449,448,1,0,65,64,129,128,193,192},{259,258,32..., dimensions={0} | all-to-all | bytes 16384 | tf_op jit(solution)/shard_map/all_to_all | solution.py:279
  112.6 10.6 %all_to_all.39.got_ref = f32[32,1,128]{2,1,0:T(1,128)S(1)} all-to-all(f32[32,1,128]{2,1,0:T(1,128)S(1)} %shard_map.56), channel_id=1, replica_groups={{36,38,32,34,44,46,40,42,52,54,48,50,60,62,56,58,4,6,0,2,12,14,8,10,20,..., dimensions={0} | all-to-all | bytes 32768 | tf_op jit(solution)/shard_map/all_to_all | solution.py:279
  123.2 0.7 shard_map.57
  (1 shorter events, 0.0 us)
Async XLA Ops:
  0.6 61.7 %copy-start = (f32[96,64]{0,1:T(8,128)S(1)}, f32[96,64]{0,1:T(8,128)}, u32[]{:S(2)}) copy-start(f32[96,64]{0,1:T(8,128)} %param.3) | copy-start | bytes 73732
  2.4 29.4 %all-to-all-start = ((f32[16,56,128]{2,1,0:T(8,128)}), f32[16,56,128]{2,1,0:T(8,128)S(1)}, u32[]{:S(2)}, u32[]{:S(2)}) async-start(f32[16,56,128]{2,1,0:T(8,128)} %get-tuple-element.16), calls=%async_computation | async-start | bytes 917504 | tf_op jit(solution)/shard_map/all_to_all | solution.py:279
  31.8 11.7 %all-to-all-start.1 = ((f32[16,8,128]{2,1,0:T(8,128)}), f32[16,8,128]{2,1,0:T(8,128)S(1)}, u32[]{:S(2)}, u32[]{:S(2)}) async-start(f32[16,8,128]{2,1,0:T(8,128)} %get-tuple-element.19), calls=%async_computation.1 | async-start | bytes 131072 | tf_op jit(solution)/shard_map/all_to_all | solution.py:279
